TPU v7x, 256 devices: a whole 4x4x8 slice. The times are simulated.
256 devices in a mesh: vv: 16 (over y, z_lo, core), oo: 16 (over x, z_hi).
Axes of the slice: x: 4, y: 4, z: 8 (z_hi: 4, z_lo: 2; z = z_hi * 2 + z_lo), core: 2. Of those that a mesh axis runs over, the one named last changes fastest.
Arguments:
- integrals: bfloat16 [16384, 256], P('vv', 'oo'), may hold values from -0.375 to 0.375
- amplitudes: bfloat16 [256, 16384], P('vv', 'oo'), may hold values from -6 to 6
- occ_energy: float32 [128], replicated, may hold values from -2 to -0.3
- vir_energy: float32 [128], replicated, may hold values from 0.1 to 3
Outputs:
- update: bfloat16 [16384, 16384], P('vv', 'oo')
All inputs are finite; a program needn't handle non-finite values.
Results may differ from a plain program's by a relative error of at most 0.0085.
Values may be sent and summed in bfloat16 or wider, within the bound.
A program may use at most 64 MiB of HBM per device.

v0:
```python
import jax
import jax.numpy as jnp
from jax import lax
from jax.sharding import PartitionSpec as P


def sent_to_all(array, axis):
    copies = jnp.broadcast_to(array, (lax.axis_size(axis), *array.shape))
    return lax.all_to_all(copies, axis, split_axis=0, concat_axis=0, tiled=True)


def joined_along(pieces, dim):
    pieces = jnp.moveaxis(pieces, 0, dim)
    dims = pieces.shape
    return pieces.reshape(*dims[:dim], dims[dim] * dims[dim + 1], *dims[dim + 2 :])


def gather_directly(array, axis, dim):
    pieces = sent_to_all(array, axis)
    return joined_along(pieces, dim)


def sent_together(arrays, axis, dim, along):
    ends, at = ([], 0)
    for a in arrays[:-1]:
        at += a.shape[along]
        ends.append(at)
    both = jnp.concatenate(arrays, axis=along)
    return tuple(jnp.split(gather_directly(both, axis, dim), ends, axis=along))


def on_device(integrals, amplitudes, occ_energy, vir_energy):
    vir_all = vir_energy.shape[0]
    occ_all = occ_energy.shape[0]
    vir_local = vir_all // lax.axis_size("vv")
    occ_local = occ_all // lax.axis_size("oo")
    row_count = vir_local * vir_all
    col_count = occ_local * occ_all
    cd_oo = integrals.shape[1]
    cd_vv = amplitudes.shape[0]
    int_moved = lax.all_to_all(
        integrals.reshape(vir_local, vir_all, cd_oo), "vv", split_axis=1, concat_axis=0, tiled=True
    )
    int_mirror = jnp.transpose(int_moved, (1, 0, 2)).reshape(row_count, cd_oo)
    amp_moved = lax.all_to_all(
        amplitudes.reshape(cd_vv, occ_local, occ_all), "oo", split_axis=2, concat_axis=1, tiled=True
    )
    amp_mirror = jnp.transpose(amp_moved, (0, 2, 1)).reshape(cd_vv, col_count)
    amp_full, mirror_full = sent_together((amplitudes, amp_mirror), "vv", 0, 1)
    int_full, int_flip = sent_together((integrals, int_mirror), "oo", 1, 0)
    direct_sum = jnp.dot(int_full, amp_full, preferred_element_type=jnp.float32)
    ladder = direct_sum.astype(jnp.bfloat16).reshape(vir_local, vir_all, occ_local, occ_all)
    mirror_sum = jnp.dot(int_flip, mirror_full, preferred_element_type=jnp.float32)
    mirrored = mirror_sum.astype(jnp.bfloat16).reshape(vir_local, vir_all, occ_local, occ_all)
    vir_mine = lax.dynamic_slice_in_dim(vir_energy, lax.axis_index("vv") * vir_local, vir_local, 0)
    occ_mine = lax.dynamic_slice_in_dim(occ_energy, lax.axis_index("oo") * occ_local, occ_local, 0)
    denom = (
        occ_mine[None, None, :, None]
        + occ_energy[None, None, None, :]
        - vir_mine[:, None, None, None]
        - vir_energy[None, :, None, None]
    )
    total = ladder.astype(jnp.float32) + mirrored.astype(jnp.float32)
    return (total / denom).astype(jnp.bfloat16).reshape(row_count, col_count)


def solution(mesh):
    placed = (P("vv", "oo"), P("vv", "oo"), P(), P())
    return jax.shard_map(
        on_device, mesh=mesh, in_specs=placed, out_specs=P("vv", "oo"), check_vma=False
    )
```

profile of v0, /device:TPU:1, one launch (start us, length us, event | category | flops | bytes accessed | tf_op | source)
XLA Modules:
  0.0 93.8 jit_solution(10716603225030355054)
XLA Ops:
  0.0 0.8 copy.34
  0.8 0.2 copy.24
  1.0 0.9 reshape.68
  1.9 7.3 %all-to-all-start = ((bf16[16,2,512]{2,1,0:T(2,128)(2,1)}), bf16[16,2,512]{2,1,0:T(2,128)(2,1)S(1)}, u32[]{:S(2)}, u32[]{:S(2)}) async-start(bf16[16,2,512]{2,1,0:T(2,128)(2,1)} %reshape.68), calls=%async_computation | async-start | bytes 65536 | tf_op jit(solution)/shard_map/all_to_all | solution.py:41
  9.2 0.8 copy.36
  10.0 0.2 copy.28
  10.2 0.9 reshape.70
  11.1 4.0 %all-to-all-done = bf16[16,2,512]{2,1,0:T(2,128)(2,1)S(1)} async-done(((bf16[16,2,512]{2,1,0:T(2,128)(2,1)}), bf16[16,2,512]{2,1,0:T(2,128)(2,1)S(1)}, u32[]{:S(2)}, u32[]{:S(2)}) %all-to-all-start) | async-done | bytes 32800 | tf_op jit(solution)/shard_map/all_to_all | solution.py:41
  15.0 9.9 %all-to-all-start.2 = ((bf16[16,2,512]{2,1,0:T(2,128)(2,1)}), bf16[16,2,512]{2,1,0:T(2,128)(2,1)S(1)}, u32[]{:S(2)}, u32[]{:S(2)}) async-start(bf16[16,2,512]{2,1,0:T(2,128)(2,1)} %reshape.70), calls=%async_computation.2 | async-start | bytes 65536 | tf_op jit(solution)/shard_map/all_to_all | solution.py:45
  24.9 0.2 reshape.69
  25.2 0.0 copy-start.2
  25.2 0.0 copy-start.1
  25.2 0.2 copy.27
  25.4 0.8 pad_maximum_fusion
  26.2 7.6 %all-to-all-done.2 = bf16[16,2,512]{2,1,0:T(2,128)(2,1)S(1)} async-done(((bf16[16,2,512]{2,1,0:T(2,128)(2,1)}), bf16[16,2,512]{2,1,0:T(2,128)(2,1)S(1)}, u32[]{:S(2)}, u32[]{:S(2)}) %all-to-all-start.2) | async-done | bytes 32800 | tf_op jit(solution)/shard_map/all_to_all | solution.py:45
  33.7 1.1 %broadcast_in_dim.4 = bf16[16,2048,16]{1,2,0:T(8,128)(2,1)} broadcast(bf16[2048,16]{0,1:T(8,128)(2,1)S(1)} %pad_maximum_fusion), dimensions={1,2} | broadcast | bytes 1114112 | tf_op jit(solution)/shard_map/broadcast_in_dim | solution.py:8
  34.8 3.7 %all-to-all-start.1 = ((bf16[16,2048,16]{1,2,0:T(8,128)(2,1)}), bf16[16,2048,16]{1,2,0:T(8,128)(2,1)S(1)}, u32[]{:S(2)}, u32[]{:S(2)}) async-start(bf16[16,2048,16]{1,2,0:T(8,128)(2,1)} %broadcast_in_dim.4), calls=%async_computation.1 | async-start | bytes 2097152 | tf_op jit(solution)/shard_map/all_to_all | solution.py:9
  38.5 0.2 reshape.71
  38.8 0.2 copy.31
  39.0 26.3 %all-to-all-done.1 = bf16[16,2048,16]{1,2,0:T(8,128)(2,1)S(1)} async-done(((bf16[16,2048,16]{1,2,0:T(8,128)(2,1)}), bf16[16,2048,16]{1,2,0:T(8,128)(2,1)S(1)}, u32[]{:S(2)}, u32[]{:S(2)}) %all-to-all-start.1) | async-done | bytes 1048608 | tf_op jit(solution)/shard_map/all_to_all | solution.py:9
  65.3 1.1 %broadcast_in_dim.5 = bf16[16,16,2048]{2,1,0:T(8,128)(2,1)} broadcast(bf16[16,2048]{1,0:T(8,128)(2,1)S(1)} %pad_maximum_fusion.1), dimensions={1,2} | broadcast | bytes 1114112 | tf_op jit(solution)/shard_map/broadcast_in_dim | solution.py:8
  66.4 7.8 %all-to-all-start.3 = ((bf16[16,16,2048]{2,1,0:T(8,128)(2,1)}), bf16[16,16,2048]{2,1,0:T(8,128)(2,1)S(1)}, u32[]{:S(2)}, u32[]{:S(2)}) async-start(bf16[16,16,2048]{2,1,0:T(8,128)(2,1)} %broadcast_in_dim.5), calls=%async_computation.3 | async-start | bytes 2097152 | tf_op jit(solution)/shard_map/all_to_all | solution.py:9
  74.1 0.1 dynamic_slice.6
  74.2 0.0 copy-done.1
  74.2 0.1 dynamic_slice.7
  74.3 0.1 broadcast_add_fusion
  74.3 0.1 broadcast_subtract_fusion
  74.4 0.1 fusion.5
  74.5 15.5 %all-to-all-done.3 = bf16[16,16,2048]{2,1,0:T(8,128)(2,1)S(1)} async-done(((bf16[16,16,2048]{2,1,0:T(8,128)(2,1)}), bf16[16,16,2048]{2,1,0:T(8,128)(2,1)S(1)}, u32[]{:S(2)}, u32[]{:S(2)}) %all-to-all-start.3) | async-done | bytes 1048608 | tf_op jit(solution)/shard_map/all_to_all | solution.py:9
  90.0 0.7 fusion.3
  90.8 0.3 sub.41
  91.1 2.7 %fusion.1 = bf16[1024,1024]{1,0:T(8,128)(2,1)} fusion(f32[128,8,8,128]{3,2,1,0:T(8,128)S(1)} %bitcast.48, f32[1024]{0:T(1024)S(1)} %broadcast_bitcast_fusion, bf16[1024,1024]{1,0:T(8,128)(2,1)S(1)} %fusion.3, bf16[1024,256]{0,1:T(8,128)(2,1)S(1)} %bitcast.59, bf16[256,2048]{1,0:T(8,128)(2,1)S(1)} %bitcast.51), kind=kOutput, calls=%fused_computation.2 | convolution fusion | flops 544210944 | bytes 9441280 | tf_op jit(solution)/shard_map/dot_general | solution.py:53
  (9 shorter events, 0.1 us)
Async XLA Ops:
  0.0 39.0 %copy-start = (bf16[16,1024]{1,0:T(8,128)(2,1)S(1)}, bf16[16,1024]{1,0:T(8,128)(2,1)}, u32[]{:S(2)}) copy-start(bf16[16,1024]{1,0:T(8,128)(2,1)} %param.5) | copy-start | bytes 98308
  1.9 13.1 %all-to-all-start = ((bf16[16,2,512]{2,1,0:T(2,128)(2,1)}), bf16[16,2,512]{2,1,0:T(2,128)(2,1)S(1)}, u32[]{:S(2)}, u32[]{:S(2)}) async-start(bf16[16,2,512]{2,1,0:T(2,128)(2,1)} %reshape.68), calls=%async_computation | async-start | bytes 65536 | tf_op jit(solution)/shard_map/all_to_all | solution.py:41
  15.0 18.7 %all-to-all-start.2 = ((bf16[16,2,512]{2,1,0:T(2,128)(2,1)}), bf16[16,2,512]{2,1,0:T(2,128)(2,1)S(1)}, u32[]{:S(2)}, u32[]{:S(2)}) async-start(bf16[16,2,512]{2,1,0:T(2,128)(2,1)} %reshape.70), calls=%async_computation.2 | async-start | bytes 65536 | tf_op jit(solution)/shard_map/all_to_all | solution.py:45
  25.2 49.0 %copy-start.2 = (f32[128]{0:T(128)S(1)}, f32[128]{0:T(128)}, u32[]{:S(2)}) copy-start(f32[128]{0:T(128)} %param.6) | copy-start | bytes 1540
  25.2 49.0 %copy-start.1 = (f32[128]{0:T(128)S(1)}, f32[128]{0:T(128)}, u32[]{:S(2)}) copy-start(f32[128]{0:T(128)} %param.7) | copy-start | bytes 1540
  34.8 30.4 %all-to-all-start.1 = ((bf16[16,2048,16]{1,2,0:T(8,128)(2,1)}), bf16[16,2048,16]{1,2,0:T(8,128)(2,1)S(1)}, u32[]{:S(2)}, u32[]{:S(2)}) async-start(bf16[16,2048,16]{1,2,0:T(8,128)(2,1)} %broadcast_in_dim.4), calls=%async_computation.1 | async-start | bytes 2097152 | tf_op jit(solution)/shard_map/all_to_all | solution.py:9
  66.4 23.7 %all-to-all-start.3 = ((bf16[16,16,2048]{2,1,0:T(8,128)(2,1)}), bf16[16,16,2048]{2,1,0:T(8,128)(2,1)S(1)}, u32[]{:S(2)}, u32[]{:S(2)}) async-start(bf16[16,16,2048]{2,1,0:T(8,128)(2,1)} %broadcast_in_dim.5), calls=%async_computation.3 | async-start | bytes 2097152 | tf_op jit(solution)/shard_map/all_to_all | solution.py:9
where the time goes:
time: 94.3 us; the launch traced here: 93.8 us
  waiting for transfers between devices  53.3 us (57%)
  starting transfers between devices  28.6 us (30%)
  local copies, waits for them, and re-layouts  7.33 us (8%)
  matrix products  3.45 us (4%)
    all_to_all x2, waiting for transfers between devices, sent_to_all(): return lax.all_to_all(copies, axis, split_axis=0, concat_axis=0, tiled=True)  41.8 us
    all_to_all x2, starting transfers between devices, sent_to_all(): return lax.all_to_all(copies, axis, split_axis=0, concat_axis=0, tiled=True)  11.4 us
    all_to_all x1, starting transfers between devices, on_device(): lax.all_to_all(amplitudes.reshape(cd_vv, occ_local, occ_all), 'oo', split...  9.85 us
    all_to_all x1, waiting for transfers between devices, on_device(): lax.all_to_all(amplitudes.reshape(cd_vv, occ_local, occ_all), 'oo', split...  7.58 us
    all_to_all x1, starting transfers between devices, on_device(): lax.all_to_all(integrals.reshape(vir_local, vir_all, cd_oo), 'vv', split_...  7.34 us
    all_to_all x1, waiting for transfers between devices, on_device(): lax.all_to_all(integrals.reshape(vir_local, vir_all, cd_oo), 'vv', split_...  3.96 us
    unnamed x14, local copies, waits for them, and re-layouts  3.77 us
    dot_general x1, matrix products, on_device(): jnp.dot(int_flip, mirror_full, preferred_element_type=jnp.float32)  2.71 us
  transfers between devices with their start and end apart: 4, of which 4 were waited for; matrix products, arithmetic and copies ran while one was open for 4% of the time, Pallas kernels for 0%

commit v1 on v0

v1 whole, which is shorter than its diff:
```python
import functools

import jax
import jax.numpy as jnp
from jax import lax
from jax.experimental import pallas as pl
from jax.experimental.pallas import tpu as pltpu
from jax.sharding import PartitionSpec as P

MESH = pl.DeviceIdType.MESH
GROUP = 16
CDS = 16
OWN = 8
ORB = 128
WIDE = OWN * ORB
CD = GROUP * CDS


def ring(at, step, size):
    return lax.rem(at + step, size)


def slot(kind, owner):
    return pl.ds(pl.multiple_of(kind * CD + owner * CDS, CDS), CDS)


def split_by_partner(chunk, turn, pieces):
    for j in range(OWN):
        turn[pl.ds(j, CDS, stride=OWN), :] = chunk[:, j * ORB : (j + 1) * ORB].astype(jnp.float32)
    pieces[...] = turn[...].T.reshape(GROUP, OWN, ORB)


def join_from_partners(pieces, turn, chunk):
    rows = [pieces[p] for p in range(GROUP)]
    group = lax.broadcasted_iota(jnp.int32, (OWN, ORB), 1) // OWN
    for bit in (1, 2, 4, 8):
        high = (group & bit) != 0
        for low in range(GROUP):
            if low & bit == 0:
                first, second = rows[low], rows[low + bit]
                rows[low] = jnp.where(high, pltpu.roll(second, bit * OWN, 1), first)
                rows[low + bit] = jnp.where(high, second, pltpu.roll(first, ORB - bit * OWN, 1))
    for c in range(CDS):
        turn[c * OWN : (c + 1) * OWN, :] = rows[c]
    for i in range(OWN):
        chunk[:, i * ORB : (i + 1) * ORB] = turn[pl.ds(i, CDS, stride=OWN), :].astype(chunk.dtype)


def gather_kernel(
    int_in, amp_in, int_all, amp_all,
    int_out_pieces, int_in_pieces, amp_out_pieces, amp_in_pieces, turn,
    local_sem, pair_send, pair_recv, int_send, int_recv, amp_send, amp_recv,
):
    vv, oo = lax.axis_index("vv"), lax.axis_index("oo")
    y, z_lo, core = vv // 4, (vv // 2) % 2, vv % 2
    x, z_hi = oo // 4, oo % 4

    barrier = pltpu.get_barrier_semaphore()
    loads = [
        pltpu.make_async_copy(int_in, int_all.at[slot(0, oo)], local_sem.at[0]),
        pltpu.make_async_copy(amp_in, amp_all.at[slot(0, vv)], local_sem.at[1]),
    ]
    for load in loads:
        load.start()
    for k in range(1, GROUP):
        pl.semaphore_signal(barrier, inc=1, device_id=(ring(vv, k, GROUP), oo), device_id_type=MESH)
        pl.semaphore_signal(barrier, inc=1, device_id=(vv, ring(oo, k, GROUP)), device_id_type=MESH)
    for load in loads:
        load.wait()

    split_by_partner(int_all.at[slot(0, oo)], turn.at[0], int_out_pieces)
    split_by_partner(amp_all.at[slot(0, vv)], turn.at[1], amp_out_pieces)
    int_in_pieces[vv] = int_out_pieces[vv]
    amp_in_pieces[oo] = amp_out_pieces[oo]
    pl.semaphore_wait(barrier, 2 * (GROUP - 1))

    sent = []

    def send(src, dst, send_sem, recv_sem, device):
        copy = pltpu.make_async_remote_copy(
            src_ref=src, dst_ref=dst, send_sem=send_sem, recv_sem=recv_sem,
            device_id=device, device_id_type=MESH,
        )
        copy.start()
        sent.append(copy)

    used = {"int": 0, "amp": 0}

    def send_int(kind, owner, device):
        rows, n = slot(kind, owner), used["int"]
        used["int"] += 1
        send(int_all.at[rows], int_all.at[rows], int_send.at[n], int_recv.at[kind, owner], device)

    def send_amp(kind, owner, device):
        rows, n = slot(kind, owner), used["amp"]
        used["amp"] += 1
        send(amp_all.at[rows], amp_all.at[rows], amp_send.at[n], amp_recv.at[kind, owner], device)

    def wait_for(array, kind, owner, recv_sem):
        rows = array.at[slot(kind, owner)]
        pltpu.make_async_copy(rows, rows, recv_sem.at[kind, owner]).wait()

    x_peers = [ring(x, k, 4) for k in (1, 3, 2)]
    z_peers = [ring(z_hi, k, 4) for k in (1, 3, 2)]
    y_peers = [ring(y, k, 4) for k in (1, 3, 2)]

    def spread_int(kind):
        for z in z_peers:
            send_int(kind, oo, (vv, x * 4 + z))
        for other in x_peers:
            send_int(kind, oo, (vv, other * 4 + z_hi))

    def spread_amp(kind):
        send_amp(kind, vv, (vv + 2 - 4 * z_lo, oo))
        for other in y_peers:
            send_amp(kind, vv, (other * 4 + z_lo * 2 + core, oo))
        send_amp(kind, vv, (vv + 1 - 2 * core, oo))

    spread_int(0)
    spread_amp(0)
    for k in range(1, GROUP):
        v, o = ring(vv, k, GROUP), ring(oo, k, GROUP)
        send(int_out_pieces.at[v], int_in_pieces.at[vv], pair_send.at[0, k], pair_recv.at[0, vv], (v, oo))
        send(amp_out_pieces.at[o], amp_in_pieces.at[oo], pair_send.at[1, k], pair_recv.at[1, oo], (vv, o))
    for k in range(1, GROUP):
        v = ring(vv, k, GROUP)
        pltpu.make_async_copy(int_in_pieces.at[v], int_in_pieces.at[v], pair_recv.at[0, v]).wait()
    join_from_partners(int_in_pieces, turn.at[0], int_all.at[slot(1, oo)])
    spread_int(1)
    for k in range(1, GROUP):
        o = ring(oo, k, GROUP)
        pltpu.make_async_copy(amp_in_pieces.at[o], amp_in_pieces.at[o], pair_recv.at[1, o]).wait()
    join_from_partners(amp_in_pieces, turn.at[1], amp_all.at[slot(1, vv)])
    spread_amp(1)

    neighbour = vv + 2 - 4 * z_lo
    sibling = vv + 1 - 2 * core
    for kind in range(2):
        for z in z_peers:
            wait_for(int_all, kind, x * 4 + z, int_recv)
            for other in x_peers:
                send_int(kind, x * 4 + z, (vv, other * 4 + z_hi))
        wait_for(amp_all, kind, neighbour, amp_recv)
        for other in y_peers:
            send_amp(kind, neighbour, (other * 4 + z_lo * 2 + core, oo))
        send_amp(kind, neighbour, (sibling, oo))
    for kind in range(2):
        for other in y_peers:
            for z in (z_lo, 1 - z_lo):
                owner = other * 4 + z * 2 + core
                wait_for(amp_all, kind, owner, amp_recv)
                send_amp(kind, owner, (sibling, oo))
    for kind in range(2):
        for far in range(8):
            wait_for(amp_all, kind, far * 2 + 1 - core, amp_recv)
        for other in x_peers:
            for z in range(4):
                wait_for(int_all, kind, other * 4 + z, int_recv)
    for copy in sent:
        copy.wait_send()


def gathered(integrals_t, amplitudes):
    whole = pltpu.VMEM((2 * CD, WIDE), jnp.bfloat16)
    pieces = pltpu.VMEM((GROUP, OWN, ORB), jnp.float32)
    return pl.pallas_call(
        gather_kernel,
        out_shape=(whole, whole),
        in_specs=[pl.BlockSpec(memory_space=pl.ANY)] * 2,
        out_specs=(pl.BlockSpec(memory_space=pltpu.VMEM),) * 2,
        scratch_shapes=[
            pieces, pieces, pieces, pieces,
            pltpu.VMEM((2, ORB, ORB), jnp.float32),
            pltpu.SemaphoreType.DMA((2,)),
            pltpu.SemaphoreType.DMA((2, GROUP)),
            pltpu.SemaphoreType.DMA((2, GROUP)),
            pltpu.SemaphoreType.DMA((30,)),
            pltpu.SemaphoreType.DMA((2, GROUP)),
            pltpu.SemaphoreType.DMA((30,)),
            pltpu.SemaphoreType.DMA((2, GROUP)),
        ],
        compiler_params=pltpu.CompilerParams(
            collective_id=0, has_side_effects=True, vmem_limit_bytes=16 << 20
        ),
        name="gather_pairs",
    )(integrals_t, amplitudes)


ROWS = 256


def ladder_kernel(int_ref, amp_ref, occ_ref, vir_ref, occ_mine, vir_mine, out_ref):
    step = pl.program_id(0)
    total = lax.dot_general(
        int_ref[...], amp_ref[...], (((0,), (0,)), ((), ())), preferred_element_type=jnp.float32
    )
    pieces = []
    for a in range(ROWS // ORB):
        vir_pair = vir_mine[step * (ROWS // ORB) + a] + vir_ref[...]
        for i in range(OWN):
            denom = (occ_mine[i] + occ_ref[...]) - vir_pair
            block = total[a * ORB : (a + 1) * ORB, i * ORB : (i + 1) * ORB] / denom
            out_ref[a * ORB : (a + 1) * ORB, i * ORB : (i + 1) * ORB] = block.astype(out_ref.dtype)


def ladder(int_all, amp_all, occ_energy, vir_energy, occ_mine, vir_mine):
    smem = pl.BlockSpec(memory_space=pltpu.SMEM)
    return pl.pallas_call(
        ladder_kernel,
        grid=(WIDE // ROWS,),
        out_shape=jax.ShapeDtypeStruct((WIDE, WIDE), jnp.bfloat16),
        in_specs=[
            pl.BlockSpec((2 * CD, ROWS), lambda s: (0, s)),
            pl.BlockSpec((2 * CD, WIDE), lambda s: (0, 0)),
            pl.BlockSpec((1, ORB), lambda s: (0, 0)),
            pl.BlockSpec((ORB, 1), lambda s: (0, 0)),
            smem,
            smem,
        ],
        out_specs=pl.BlockSpec((ROWS, WIDE), lambda s: (s, 0)),
        compiler_params=pltpu.CompilerParams(vmem_limit_bytes=32 << 20),
        name="ladder_sum",
    )(int_all, amp_all, occ_energy.reshape(1, ORB), vir_energy.reshape(ORB, 1), occ_mine, vir_mine)


def on_device(integrals, amplitudes, occ_energy, vir_energy):
    int_all, amp_all = gathered(integrals.T, amplitudes)
    occ_mine = lax.dynamic_slice_in_dim(occ_energy, lax.axis_index("oo") * OWN, OWN, 0)
    vir_mine = lax.dynamic_slice_in_dim(vir_energy, lax.axis_index("vv") * OWN, OWN, 0)
    return ladder(int_all, amp_all, occ_energy, vir_energy, occ_mine, vir_mine)


def solution(mesh):
    placed = (P("vv", "oo"), P("vv", "oo"), P(), P())
    return jax.shard_map(
        on_device, mesh=mesh, in_specs=placed, out_specs=P("vv", "oo"), check_vma=False
    )
```

time: 94.3 us -> 41.8 us (0.44)
  waiting for transfers between devices: 53.3 us -> 0 us
  Pallas kernels: 0 us -> 37.1 us
  starting transfers between devices: 28.6 us -> 0 us
  matrix products: 3.45 us -> 0 us
  local copies, waits for them, and re-layouts: 7.33 us -> 4.38 us
    all_to_all x4 -> x0, waiting for transfers between devices: 53.3 us -> none  [the longest x2 41.8 us: sent_to_all(): return lax.all_to_all(copies, axis, split_axis=0, concat_axis=0, tiled=True)]
    pallas_call x0 -> x2, Pallas kernels: none -> 37.1 us  [the longest x1 33.5 us: gathered(): pl.pallas_call(gather_kernel, out_shape=(whole, whole), in_specs=[pl.Bloc...]
    all_to_all x4 -> x0, starting transfers between devices: 28.6 us -> none  [the longest x2 11.4 us: sent_to_all(): return lax.all_to_all(copies, axis, split_axis=0, concat_axis=0, tiled=True)]
    dot_general x2 -> x0, matrix products: 3.45 us -> none  [the longest x1 2.71 us: on_device(): jnp.dot(int_flip, mirror_full, preferred_element_type=jnp.float32)]
    broadcast_in_dim x2 -> x0, local copies, waits for them, and re-layouts: 2.18 us -> none  [sent_to_all(): copies = jnp.broadcast_to(array, (lax.axis_size(axis), *array.shape))]
    unnamed x14 -> x6, local copies, waits for them, and re-layouts: 3.77 us -> 2.16 us
    dynamic_slice x2, local copies, waits for them, and re-layouts: 0.15 us -> 1.45 us  [the longest x1 0.73 us: on_device(): lax.dynamic_slice_in_dim(vir_energy, lax.axis_index('vv') * OWN, OWN, 0)]
  transfers between devices with their start and end apart: 4 -> 0, of which waited for: 4 -> 0; matrix products, arithmetic and copies ran while one was open for 4% -> 0% of each run, Pallas kernels for 0% -> 0%
where the time goes in v1:
time: 41.8 us; the launch traced here: 41.5 us
  Pallas kernels  37.1 us (89%)
  local copies, waits for them, and re-layouts  4.38 us (10%)
    pallas_call x1, Pallas kernels, gathered(): pl.pallas_call(gather_kernel, out_shape=(whole, whole), in_specs=[pl.Bloc...  33.5 us
    pallas_call x1, Pallas kernels, ladder(): pl.pallas_call(ladder_kernel, grid=(WIDE // ROWS,), out_shape=jax.ShapeDt...  3.63 us
    unnamed x6, local copies, waits for them, and re-layouts  2.16 us

profile of v1, /device:TPU:1, one launch (start us, length us, event | category | flops | bytes accessed | tf_op | source)
XLA Modules:
  0.0 41.5 jit_solution(6260337733160412481)
XLA Ops:
  0.0 0.7 %dynamic_slice.6.occ_mine = f32[8]{0:T(128)S(1)} dynamic-slice(f32[128]{0:T(128)} %param.6, s32[]{:T(128)S(6)} %select_n.6), dynamic_slice_sizes={8} | dynamic-slice | bytes 68 | tf_op jit(solution)/shard_map/dynamic_slice | solution.py:228
  0.7 0.7 %dynamic_slice.7.vir_mine = f32[8]{0:T(128)S(1)} dynamic-slice(f32[128]{0:T(128)} %param.7, s32[]{:T(128)S(6)} %select_n.7), dynamic_slice_sizes={8} | dynamic-slice | bytes 68 | tf_op jit(solution)/shard_map/dynamic_slice | solution.py:229
  1.5 0.8 %copy.5.vir_ref = f32[128,1]{1,0:T(8,128)S(1)} copy(f32[128,1]{0,1:T(1,128)} %bitcast.5) | data formatting | bytes 1024 | tf_op jit(solution)/shard_map/reshape | solution.py:223
  2.2 0.0 copy-start
  2.2 0.8 %copy-done = bf16[1024,16]{0,1:T(8,128)(2,1)S(1)} copy-done((bf16[1024,16]{0,1:T(8,128)(2,1)S(1)}, bf16[1024,16]{0,1:T(8,128)(2,1)}, u32[]{:S(2)}) %copy-start) | copy-done | bytes 32792
  3.0 0.0 copy-start.1
  3.0 0.8 %copy-done.1 = bf16[16,1024]{1,0:T(8,128)(2,1)S(1)} copy-done((bf16[16,1024]{1,0:T(8,128)(2,1)S(1)}, bf16[16,1024]{1,0:T(8,128)(2,1)}, u32[]{:S(2)}) %copy-start.1) | copy-done | bytes 32792
  3.7 33.5 %gather_pairs.1 = (bf16[512,1024]{1,0:T(8,128)(2,1)S(1)}, bf16[512,1024]{1,0:T(8,128)(2,1)S(1)}) custom-call(bf16[16,1024]{1,0:T(8,128)(2,1)S(1)} %bitcast.3, bf16[16,1024]{1,0:T(8,128)(2,1)S(1)} %copy-done.1), custom_call_target="tpu_custom_call" | custom-call | tf_op jit(solution)/shard_map/gather_pairs/pallas_call | solution.py:166
  37.2 0.0 copy-start.2
  37.3 0.6 %copy-done.2 = f32[128]{0:T(128)S(1)} copy-done((f32[128]{0:T(128)S(1)}, f32[128]{0:T(128)}, u32[]{:S(2)}) %copy-start.2) | copy-done | bytes 536
  37.9 3.6 %ladder_sum.1 = bf16[1024,1024]{1,0:T(8,128)(2,1)} custom-call(bf16[512,1024]{1,0:T(8,128)(2,1)S(1)} %get-tuple-element.7.int_ref, bf16[512,1024]{1,0:T(8,128)(2,1)S(1)} %get-tuple-element.8.amp_ref, f32[1,128]{1,0:T(1,128)S(1)} %bitcast.4, f32[128,1]{1,0:T(8,128)S(1)} %copy.5.vir_ref, f32[8]{0:T(128)S(1)} %dynamic_slice.6.occ_mine, f32[8]{0:T(128)S(1)} %dynamic_slice.7.vir_mine), custom_call_target="tpu_custom_call" | custom-call | tf_op jit(solution)/shard_map/ladder_sum/pallas_call | solution.py:208
Async XLA Ops:
  2.2 0.8 %copy-start = (bf16[1024,16]{0,1:T(8,128)(2,1)S(1)}, bf16[1024,16]{0,1:T(8,128)(2,1)}, u32[]{:S(2)}) copy-start(bf16[1024,16]{0,1:T(8,128)(2,1)} %param.4) | copy-start | bytes 98308
  3.0 0.8 %copy-start.1 = (bf16[16,1024]{1,0:T(8,128)(2,1)S(1)}, bf16[16,1024]{1,0:T(8,128)(2,1)}, u32[]{:S(2)}) copy-start(bf16[16,1024]{1,0:T(8,128)(2,1)} %amp_in.1) | copy-start | bytes 98308
  37.2 0.7 %copy-start.2 = (f32[128]{0:T(128)S(1)}, f32[128]{0:T(128)}, u32[]{:S(2)}) copy-start(f32[128]{0:T(128)} %param.6) | copy-start | bytes 1540

commit v2 on v1

v2 whole, which is shorter than its diff:
```python
import jax
import jax.numpy as jnp
from jax import lax
from jax.experimental import pallas as pl
from jax.experimental.pallas import tpu as pltpu
from jax.sharding import PartitionSpec as P

MESH = pl.DeviceIdType.MESH
GROUP = 16
CDS = 16
OWN = 8
ORB = 128
WIDE = OWN * ORB
CD = GROUP * CDS
RING = 4


def around(at, step):
    return (at + step + RING) % RING


def slot(kind, owner):
    return pl.ds(pl.multiple_of(kind * CD + owner * CDS, CDS), CDS)


def split_by_partner(chunk, turn, pieces):
    for j in range(OWN):
        turn[pl.ds(j, CDS, stride=OWN), :] = chunk[:, j * ORB : (j + 1) * ORB].astype(jnp.float32)
    pieces[...] = turn[...].T.reshape(pieces.shape)


def join_from_partners(rows, turn, chunk):
    group = lax.broadcasted_iota(jnp.int32, (OWN, ORB), 1) // OWN
    for bit in (1, 2, 4, 8):
        high = (group & bit) != 0
        for low in range(GROUP):
            if low & bit == 0:
                first, second = rows[low], rows[low + bit]
                rows[low] = jnp.where(high, pltpu.roll(second, bit * OWN, 1), first)
                rows[low + bit] = jnp.where(high, second, pltpu.roll(first, ORB - bit * OWN, 1))
    for c in range(CDS):
        turn[c * OWN : (c + 1) * OWN, :] = rows[c]
    for i in range(OWN):
        chunk[:, i * ORB : (i + 1) * ORB] = turn[pl.ds(i, CDS, stride=OWN), :].astype(chunk.dtype)


def gather_kernel(
    int_in, amp_in, occ_in, vir_in, int_all, amp_all, inverse,
    int_cut, int_y, int_z, int_core, amp_cut, amp_x, amp_z, amp_pass, turn,
    occ_row, vir_row, occ_at, vir_at,
    local_sem, pair_send, pair_recv, int_send, int_recv, amp_send, amp_recv,
):
    vv, oo = lax.axis_index("vv"), lax.axis_index("oo")
    y, z_lo, core = vv // 4, (vv // 2) % 2, vv % 2
    x, z_hi = oo // 4, oo % 4

    def at_y(step):
        return (around(y, step) * 4 + z_lo * 2 + core, oo)

    def at_x(step):
        return (vv, around(x, step) * 4 + z_hi)

    def at_z(step):
        return (vv, x * 4 + around(z_hi, step))

    across = (y * 4 + (1 - z_lo) * 2 + core, oo)
    sibling = (y * 4 + z_lo * 2 + 1 - core, oo)

    barrier = pltpu.get_barrier_semaphore()
    greeted = [at_z(1), at_z(-1), at_y(2), at_x(2), at_y(1), at_y(-1), at_x(1), at_x(-1), across, sibling]
    for device in greeted:
        pl.semaphore_signal(barrier, inc=1, device_id=device, device_id_type=MESH)
    loads = [
        pltpu.make_async_copy(int_in, int_all.at[slot(0, oo)], local_sem.at[0]),
        pltpu.make_async_copy(amp_in, amp_all.at[slot(0, vv)], local_sem.at[1]),
        pltpu.make_async_copy(occ_in, occ_row, local_sem.at[2]),
        pltpu.make_async_copy(vir_in, vir_row, local_sem.at[3]),
        pltpu.make_async_copy(occ_in, occ_at, local_sem.at[4]),
        pltpu.make_async_copy(vir_in, vir_at, local_sem.at[5]),
    ]
    for load in loads:
        load.start()
    for load in loads:
        load.wait()

    split_by_partner(amp_all.at[slot(0, vv)], turn.at[1], amp_cut)
    split_by_partner(int_all.at[slot(0, oo)], turn.at[0], int_cut)
    pl.semaphore_wait(barrier, len(greeted))

    sent = []

    def send(src, dst, send_sem, recv_sem, device):
        copy = pltpu.make_async_remote_copy(
            src_ref=src, dst_ref=dst, send_sem=send_sem, recv_sem=recv_sem,
            device_id=device, device_id_type=MESH,
        )
        copy.start()
        sent.append(copy)

    used = {"int": 0, "amp": 0, "pair": 0}

    def next_of(which):
        used[which] += 1
        return used[which] - 1

    def send_int(kind, owner, device):
        rows = int_all.at[slot(kind, owner)]
        send(rows, rows, int_send.at[next_of("int")], int_recv.at[kind, owner], device)

    def send_amp(kind, owner, device):
        rows = amp_all.at[slot(kind, owner)]
        send(rows, rows, amp_send.at[next_of("amp")], amp_recv.at[kind, owner], device)

    def send_pair(src, dst, arrival, device):
        send(src, dst, pair_send.at[next_of("pair")], pair_recv.at[arrival], device)

    def got(ref, sem):
        pltpu.make_async_copy(ref, ref, sem).wait()

    def got_int(kind, owner):
        got(int_all.at[slot(kind, owner)], int_recv.at[kind, owner])

    def got_amp(kind, owner):
        got(amp_all.at[slot(kind, owner)], amp_recv.at[kind, owner])

    vir_column = jnp.broadcast_to(vir_row[...], (ORB, ORB)).T

    def invert(blocks):
        for a in blocks:
            vir_pair = vir_at[0, vv * OWN + a] + vir_column
            for i in range(OWN):
                denom = (occ_at[0, oo * OWN + i] + occ_row[...]) - vir_pair
                inverse[a * ORB : (a + 1) * ORB, i * ORB : (i + 1) * ORB] = 1.0 / denom

    for step in (2, 1, -1):
        send_pair(amp_cut.at[around(x, step)], amp_x.at[x], 0 + step % RING, at_x(step))
        send_pair(int_cut.at[around(y, step)], int_y.at[y], 4 + step % RING, at_y(step))
    amp_x[x] = amp_cut[x]
    int_y[y] = int_cut[y]

    def spread_int(kind):
        for step in (1, -1):
            send_int(kind, oo, at_z(step))
        for step in (1, -1):
            send_int(kind, oo, at_x(step))

    def spread_amp(kind):
        send_amp(kind, vv, across)
        for step in (1, -1):
            send_amp(kind, vv, at_y(step))
        send_amp(kind, vv, sibling)

    def owner_int(x_step, z_step):
        return around(x, x_step) * 4 + around(z_hi, z_step)

    def owner_amp(y_step, other):
        return around(y, y_step) * 4 + (1 - z_lo if other else z_lo) * 2 + core

    def from_z(kind):
        for step in (-1, 1):
            got_int(kind, owner_int(0, step))
            if step == (-1 if kind == 0 else 1):
                send_int(kind, owner_int(0, step), at_z(-step))
            for along in (1, -1):
                send_int(kind, owner_int(0, step), at_x(along))

    def from_across(kind):
        got_amp(kind, owner_amp(0, True))
        for step in (1, -1):
            send_amp(kind, owner_amp(0, True), at_y(step))
        send_amp(kind, owner_amp(0, True), sibling)

    def from_far_z(kind):
        got_int(kind, owner_int(0, 2))
        for along in (1, -1):
            send_int(kind, owner_int(0, 2), at_x(along))

    def from_x(kind, z_step):
        up = z_step % 2 == 0
        for along in (-1, 1):
            got_int(kind, owner_int(along, z_step))
            if along == (-1 if up else 1):
                send_int(kind, owner_int(along, z_step), at_x(-along))

    def from_y(kind, other):
        for step in (-1, 1):
            got_amp(kind, owner_amp(step, other))
            if step == (1 if other else -1):
                send_amp(kind, owner_amp(step, other), at_y(-step))
            send_amp(kind, owner_amp(step, other), sibling)

    def from_far_y(kind, other):
        got_amp(kind, owner_amp(2, other))
        send_amp(kind, owner_amp(2, other), sibling)

    spread_int(0)
    spread_amp(0)

    for step in (1, -1, 2):
        got(amp_x.at[around(x, step)], pair_recv.at[0 + (-step) % RING])
    send_pair(amp_x.at[:, around(z_hi, 2)], amp_pass, 8, at_z(1))
    for step in (1, -1):
        send_pair(amp_x.at[:, around(z_hi, step)], amp_z.at[:, z_hi], 8 + step % RING if step < 0 else 9, at_z(step))
    amp_z[:, z_hi] = amp_x[:, z_hi]

    for step in (1, -1, 2):
        got(int_y.at[around(y, step)], pair_recv.at[4 + (-step) % RING])
    send_pair(int_y.at[:, 1 - z_lo], int_z.at[:, z_lo], 12, across)
    int_z[:, z_lo] = int_y[:, z_lo]
    invert(range(0, 2))

    got(int_z.at[:, 1 - z_lo], pair_recv.at[12])
    send_pair(int_z.at[:, :, 1 - core], int_core.at[:, :, core], 13, sibling)
    int_core[:, :, core] = int_z[:, :, core]

    from_z(0)
    from_across(0)
    got(amp_pass, pair_recv.at[8])
    send_pair(amp_pass, amp_z.at[:, around(z_hi, -1)], 10, at_z(1))

    got(int_core.at[:, :, 1 - core], pair_recv.at[13])
    join_from_partners(
        [int_core[p // 4, (p // 2) % 2, p % 2] for p in range(GROUP)], turn.at[0], int_all.at[slot(1, oo)]
    )
    spread_int(1)
    from_x(0, 0)
    from_y(0, False)

    got(amp_z.at[:, around(z_hi, -1)], pair_recv.at[9])
    got(amp_z.at[:, around(z_hi, 1)], pair_recv.at[11])
    got(amp_z.at[:, around(z_hi, 2)], pair_recv.at[10])
    join_from_partners([amp_z[p // 4, p % 4] for p in range(GROUP)], turn.at[1], amp_all.at[slot(1, vv)])
    spread_amp(1)

    from_far_z(0)
    from_y(0, True)
    from_x(0, -1)
    from_x(0, 1)
    invert(range(2, 4))
    from_z(1)
    from_x(0, 2)
    from_across(1)
    from_far_y(0, False)
    from_far_y(0, True)
    from_x(1, 0)
    invert(range(4, 6))
    from_y(1, False)
    from_far_z(1)
    invert(range(6, 8))
    from_x(1, -1)
    from_x(1, 1)
    from_y(1, True)
    from_x(1, 2)
    from_far_y(1, False)
    from_far_y(1, True)
    for kind in range(2):
        for z_step in range(4):
            got_int(kind, owner_int(2, z_step))
        for far in range(8):
            got_amp(kind, far * 2 + 1 - core)
    for copy in sent:
        copy.wait_send()


def gathered(integrals_t, amplitudes, occ_row, vir_row):
    whole = pltpu.VMEM((2 * CD, WIDE), jnp.bfloat16)

    def pieces(*shape):
        return pltpu.VMEM((*shape, OWN, ORB), jnp.float32)

    def dma(*shape):
        return pltpu.SemaphoreType.DMA(shape)

    held = [pltpu.with_memory_space_constraint(a, pltpu.HBM) for a in (integrals_t, amplitudes, occ_row, vir_row)]
    return pl.pallas_call(
        gather_kernel,
        out_shape=(whole, whole, pltpu.VMEM((WIDE, WIDE), jnp.float32)),
        in_specs=[pl.BlockSpec(memory_space=pltpu.HBM)] * 4,
        out_specs=(pl.BlockSpec(memory_space=pltpu.VMEM),) * 3,
        scratch_shapes=[
            pieces(4, 2, 2), pieces(4, 2, 2), pieces(4, 2, 2), pieces(4, 2, 2),
            pieces(4, 4), pieces(4, 4), pieces(4, 4), pieces(4),
            pltpu.VMEM((2, ORB, ORB), jnp.float32),
            pltpu.VMEM((1, ORB), jnp.float32), pltpu.VMEM((1, ORB), jnp.float32),
            pltpu.SMEM((1, ORB), jnp.float32), pltpu.SMEM((1, ORB), jnp.float32),
            dma(6), dma(12), dma(14), dma(38), dma(2, GROUP), dma(38), dma(2, GROUP),
        ],
        compiler_params=pltpu.CompilerParams(
            collective_id=0, has_side_effects=True, vmem_limit_bytes=32 << 20
        ),
        name="gather_pairs",
    )(*held)


ROWS = 256


def ladder_kernel(int_ref, amp_ref, inverse, out_ref, made, sems):
    copies = []
    for s in range(WIDE // ROWS):
        rows = pl.ds(s * ROWS, ROWS)
        total = lax.dot_general(
            int_ref[:, s * ROWS : (s + 1) * ROWS], amp_ref[...], (((0,), (0,)), ((), ())),
            preferred_element_type=jnp.float32,
        )
        made[rows, :] = (total * inverse[rows, :]).astype(made.dtype)
        copies.append(pltpu.make_async_copy(made.at[rows], out_ref.at[rows], sems.at[s]))
        copies[-1].start()
    for copy in copies:
        copy.wait()


def ladder(int_all, amp_all, inverse):
    return pl.pallas_call(
        ladder_kernel,
        out_shape=jax.ShapeDtypeStruct((WIDE, WIDE), jnp.bfloat16),
        in_specs=[pl.BlockSpec(memory_space=pltpu.VMEM)] * 3,
        out_specs=pl.BlockSpec(memory_space=pl.ANY),
        scratch_shapes=[
            pltpu.VMEM((WIDE, WIDE), jnp.bfloat16), pltpu.SemaphoreType.DMA((WIDE // ROWS,)),
        ],
        compiler_params=pltpu.CompilerParams(vmem_limit_bytes=32 << 20),
        name="ladder_sum",
    )(int_all, amp_all, inverse)


def on_device(integrals, amplitudes, occ_energy, vir_energy):
    return ladder(
        *gathered(integrals.T, amplitudes, occ_energy.reshape(1, ORB), vir_energy.reshape(1, ORB))
    )


def solution(mesh):
    placed = (P("vv", "oo"), P("vv", "oo"), P(), P())
    return jax.shard_map(
        on_device, mesh=mesh, in_specs=placed, out_specs=P("vv", "oo"), check_vma=False
    )
```

time: 41.8 us -> 36.7 us (0.88)
  local copies, waits for them, and re-layouts: 4.38 us -> 0 us
  Pallas kernels: 37.1 us -> 36.5 us
    unnamed x6 -> x0, local copies, waits for them, and re-layouts: 2.16 us -> none
    dynamic_slice x2 -> x0, local copies, waits for them, and re-layouts: 1.45 us -> none  [the longest x1 0.73 us: on_device(): lax.dynamic_slice_in_dim(vir_energy, lax.axis_index('vv') * OWN, OWN, 0)]
    reshape x1 -> x0, local copies, waits for them, and re-layouts: 0.76 us -> none  [ladder(): vir_energy.reshape(ORB, 1)]
    pallas_call x2, Pallas kernels: 37.1 us -> 36.5 us  [the longest x1 34.4 us: gathered(): pl.pallas_call(gather_kernel, out_shape=(whole, whole, pltpu.VMEM((WIDE,...]
where the time goes in v2:
time: 36.7 us; the launch traced here: 36.5 us
  Pallas kernels  36.5 us (99%)
    pallas_call x1, Pallas kernels, gathered(): pl.pallas_call(gather_kernel, out_shape=(whole, whole, pltpu.VMEM((WIDE,...  34.4 us
    pallas_call x1, Pallas kernels, ladder(): pl.pallas_call(ladder_kernel, out_shape=jax.ShapeDtypeStruct((WIDE, WIDE)...  2.12 us

profile of v2, /device:TPU:1, one launch (start us, length us, event | category | flops | bytes accessed | tf_op | source)
XLA Modules:
  0.0 36.5 jit_solution(14197435007869613047)
XLA Ops:
  0.0 34.4 %gather_pairs.1 = (bf16[512,1024]{1,0:T(8,128)(2,1)S(1)}, bf16[512,1024]{1,0:T(8,128)(2,1)S(1)}, f32[1024,1024]{1,0:T(8,128)S(1)}) custom-call(bf16[16,1024]{1,0:T(8,128)(2,1)} %bitcast.3, bf16[16,1024]{1,0:T(8,128)(2,1)} %amp_in.1, f32[1,128]{1,0:T(1,128)} %bitcast.4, f32[1,128]{1,0:T(1,128)} %bitcast.5), custom_call_target="tpu_custom_call" | custom-call | tf_op jit(solution)/shard_map/gather_pairs/pallas_call | solution.py:275
  34.4 2.1 %ladder_sum.1 = bf16[1024,1024]{1,0:T(8,128)(2,1)} custom-call(bf16[512,1024]{1,0:T(8,128)(2,1)S(1)} %get-tuple-element.8.int_ref, bf16[512,1024]{1,0:T(8,128)(2,1)S(1)} %get-tuple-element.9.amp_ref, f32[1024,1024]{1,0:T(8,128)S(1)} %get-tuple-element.10.inverse), custom_call_target="tpu_custom_call" | custom-call | tf_op jit(solution)/shard_map/ladder_sum/pallas_call | solution.py:314

commit v3 on v2

--- a/solution.py
+++ b/solution.py
@@ -46,7 +46,7 @@
 
 def gather_kernel(
     int_in, amp_in, occ_in, vir_in, int_all, amp_all, inverse,
-    int_cut, int_y, int_z, int_core, amp_cut, amp_x, amp_z, amp_pass, turn,
+    int_cut, int_got, amp_cut, amp_x, amp_z, turn,
     occ_row, vir_row, occ_at, vir_at,
     local_sem, pair_send, pair_recv, int_send, int_recv, amp_send, amp_recv,
 ):
@@ -63,11 +63,18 @@
     def at_z(step):
         return (vv, x * 4 + around(z_hi, step))
 
-    across = (y * 4 + (1 - z_lo) * 2 + core, oo)
+    def at_chip(y_step, other):
+        return (around(y, y_step) * 4 + (1 - z_lo if other else z_lo) * 2 + core, oo)
+
+    def at_vv(step):
+        return (lax.rem(vv + step, GROUP), oo)
+
     sibling = (y * 4 + z_lo * 2 + 1 - core, oo)
+    near = (1, -1, 2)
+    chips = [(step, other) for other in (False, True) for step in (0, *near) if step != 0 or other]
 
     barrier = pltpu.get_barrier_semaphore()
-    greeted = [at_z(1), at_z(-1), at_y(2), at_x(2), at_y(1), at_y(-1), at_x(1), at_x(-1), across, sibling]
+    greeted = [at_z(step) for step in near] + [at_x(step) for step in near] + [at_vv(step) for step in range(1, GROUP)]
     for device in greeted:
         pl.semaphore_signal(barrier, inc=1, device_id=device, device_id_type=MESH)
     loads = [
@@ -132,22 +139,15 @@
                 denom = (occ_at[0, oo * OWN + i] + occ_row[...]) - vir_pair
                 inverse[a * ORB : (a + 1) * ORB, i * ORB : (i + 1) * ORB] = 1.0 / denom
 
-    for step in (2, 1, -1):
-        send_pair(amp_cut.at[around(x, step)], amp_x.at[x], 0 + step % RING, at_x(step))
-        send_pair(int_cut.at[around(y, step)], int_y.at[y], 4 + step % RING, at_y(step))
-    amp_x[x] = amp_cut[x]
-    int_y[y] = int_cut[y]
-
     def spread_int(kind):
-        for step in (1, -1):
+        for step in near:
             send_int(kind, oo, at_z(step))
-        for step in (1, -1):
+        for step in near:
             send_int(kind, oo, at_x(step))
 
     def spread_amp(kind):
-        send_amp(kind, vv, across)
-        for step in (1, -1):
-            send_amp(kind, vv, at_y(step))
+        for step, other in chips:
+            send_amp(kind, vv, at_chip(step, other))
         send_amp(kind, vv, sibling)
 
     def owner_int(x_step, z_step):
@@ -156,106 +156,52 @@
     def owner_amp(y_step, other):
         return around(y, y_step) * 4 + (1 - z_lo if other else z_lo) * 2 + core
 
-    def from_z(kind):
-        for step in (-1, 1):
-            got_int(kind, owner_int(0, step))
-            if step == (-1 if kind == 0 else 1):
-                send_int(kind, owner_int(0, step), at_z(-step))
-            for along in (1, -1):
-                send_int(kind, owner_int(0, step), at_x(along))
-
-    def from_across(kind):
-        got_amp(kind, owner_amp(0, True))
-        for step in (1, -1):
-            send_amp(kind, owner_amp(0, True), at_y(step))
-        send_amp(kind, owner_amp(0, True), sibling)
-
-    def from_far_z(kind):
-        got_int(kind, owner_int(0, 2))
-        for along in (1, -1):
-            send_int(kind, owner_int(0, 2), at_x(along))
-
-    def from_x(kind, z_step):
-        up = z_step % 2 == 0
-        for along in (-1, 1):
-            got_int(kind, owner_int(along, z_step))
-            if along == (-1 if up else 1):
-                send_int(kind, owner_int(along, z_step), at_x(-along))
-
-    def from_y(kind, other):
-        for step in (-1, 1):
+    def onward_int(kind):
+        for z_step in near:
+            got_int(kind, owner_int(0, z_step))
+            for step in near:
+                send_int(kind, owner_int(0, z_step), at_x(step))
+
+    def onward_amp(kind):
+        for step, other in chips:
             got_amp(kind, owner_amp(step, other))
-            if step == (1 if other else -1):
-                send_amp(kind, owner_amp(step, other), at_y(-step))
             send_amp(kind, owner_amp(step, other), sibling)
 
-    def from_far_y(kind, other):
-        got_amp(kind, owner_amp(2, other))
-        send_amp(kind, owner_amp(2, other), sibling)
-
+    for step in near:
+        send_pair(amp_cut.at[around(x, step)], amp_x.at[x], step % RING, at_x(step))
+    for step in range(1, GROUP):
+        send_pair(int_cut.at[lax.rem(vv + step, GROUP)], int_got.at[vv], 8 + step, at_vv(step))
+    amp_x[x] = amp_cut[x]
+    int_got[vv] = int_cut[vv]
     spread_int(0)
     spread_amp(0)
-
-    for step in (1, -1, 2):
-        got(amp_x.at[around(x, step)], pair_recv.at[0 + (-step) % RING])
-    send_pair(amp_x.at[:, around(z_hi, 2)], amp_pass, 8, at_z(1))
-    for step in (1, -1):
-        send_pair(amp_x.at[:, around(z_hi, step)], amp_z.at[:, z_hi], 8 + step % RING if step < 0 else 9, at_z(step))
+    invert(range(0, 2))
+
+    for step in near:
+        got(amp_x.at[around(x, step)], pair_recv.at[-step % RING])
+    for step in near:
+        send_pair(amp_x.at[:, around(z_hi, step)], amp_z.at[:, z_hi], 4 + step % RING, at_z(step))
     amp_z[:, z_hi] = amp_x[:, z_hi]
 
-    for step in (1, -1, 2):
-        got(int_y.at[around(y, step)], pair_recv.at[4 + (-step) % RING])
-    send_pair(int_y.at[:, 1 - z_lo], int_z.at[:, z_lo], 12, across)
-    int_z[:, z_lo] = int_y[:, z_lo]
-    invert(range(0, 2))
-
-    got(int_z.at[:, 1 - z_lo], pair_recv.at[12])
-    send_pair(int_z.at[:, :, 1 - core], int_core.at[:, :, core], 13, sibling)
-    int_core[:, :, core] = int_z[:, :, core]
-
-    from_z(0)
-    from_across(0)
-    got(amp_pass, pair_recv.at[8])
-    send_pair(amp_pass, amp_z.at[:, around(z_hi, -1)], 10, at_z(1))
-
-    got(int_core.at[:, :, 1 - core], pair_recv.at[13])
-    join_from_partners(
-        [int_core[p // 4, (p // 2) % 2, p % 2] for p in range(GROUP)], turn.at[0], int_all.at[slot(1, oo)]
-    )
+    for step in range(1, GROUP):
+        got(int_got.at[lax.rem(vv + GROUP - step, GROUP)], pair_recv.at[8 + step])
+    join_from_partners([int_got[p] for p in range(GROUP)], turn.at[0], int_all.at[slot(1, oo)])
     spread_int(1)
-    from_x(0, 0)
-    from_y(0, False)
-
-    got(amp_z.at[:, around(z_hi, -1)], pair_recv.at[9])
-    got(amp_z.at[:, around(z_hi, 1)], pair_recv.at[11])
-    got(amp_z.at[:, around(z_hi, 2)], pair_recv.at[10])
+    invert(range(2, 3))
+    onward_int(0)
+
+    for step in near:
+        got(amp_z.at[:, around(z_hi, step)], pair_recv.at[4 + -step % RING])
     join_from_partners([amp_z[p // 4, p % 4] for p in range(GROUP)], turn.at[1], amp_all.at[slot(1, vv)])
     spread_amp(1)
-
-    from_far_z(0)
-    from_y(0, True)
-    from_x(0, -1)
-    from_x(0, 1)
-    invert(range(2, 4))
-    from_z(1)
-    from_x(0, 2)
-    from_across(1)
-    from_far_y(0, False)
-    from_far_y(0, True)
-    from_x(1, 0)
-    invert(range(4, 6))
-    from_y(1, False)
-    from_far_z(1)
-    invert(range(6, 8))
-    from_x(1, -1)
-    from_x(1, 1)
-    from_y(1, True)
-    from_x(1, 2)
-    from_far_y(1, False)
-    from_far_y(1, True)
+    onward_amp(0)
+    onward_int(1)
+    invert(range(3, 8))
+    onward_amp(1)
     for kind in range(2):
-        for z_step in range(4):
-            got_int(kind, owner_int(2, z_step))
+        for step in near:
+            for z_step in range(4):
+                got_int(kind, owner_int(step, z_step))
         for far in range(8):
             got_amp(kind, far * 2 + 1 - core)
     for copy in sent:
@@ -278,12 +224,11 @@
         in_specs=[pl.BlockSpec(memory_space=pltpu.HBM)] * 4,
         out_specs=(pl.BlockSpec(memory_space=pltpu.VMEM),) * 3,
         scratch_shapes=[
-            pieces(4, 2, 2), pieces(4, 2, 2), pieces(4, 2, 2), pieces(4, 2, 2),
-            pieces(4, 4), pieces(4, 4), pieces(4, 4), pieces(4),
+            pieces(GROUP), pieces(GROUP), pieces(4, 4), pieces(4, 4), pieces(4, 4),
             pltpu.VMEM((2, ORB, ORB), jnp.float32),
             pltpu.VMEM((1, ORB), jnp.float32), pltpu.VMEM((1, ORB), jnp.float32),
             pltpu.SMEM((1, ORB), jnp.float32), pltpu.SMEM((1, ORB), jnp.float32),
-            dma(6), dma(12), dma(14), dma(38), dma(2, GROUP), dma(38), dma(2, GROUP),
+            dma(6), dma(21), dma(8 + GROUP), dma(30), dma(2, GROUP), dma(30), dma(2, GROUP),
         ],
         compiler_params=pltpu.CompilerParams(
             collective_id=0, has_side_effects=True, vmem_limit_bytes=32 << 20

time: 36.7 us -> 33 us (0.90)
  Pallas kernels: 36.5 us -> 32.8 us
    pallas_call x1, Pallas kernels: 34.4 us -> 30.7 us  [gathered(): pl.pallas_call(gather_kernel, out_shape=(whole, whole, pltpu.VMEM((WIDE,...]
where the time goes in v3:
time: 33 us; the launch traced here: 32.8 us
  Pallas kernels  32.8 us (99%)
    pallas_call x1, Pallas kernels, gathered(): pl.pallas_call(gather_kernel, out_shape=(whole, whole, pltpu.VMEM((WIDE,...  30.7 us
    pallas_call x1, Pallas kernels, ladder(): pl.pallas_call(ladder_kernel, out_shape=jax.ShapeDtypeStruct((WIDE, WIDE)...  2.12 us

profile of v3, /device:TPU:1, one launch (start us, length us, event | category | flops | bytes accessed | tf_op | source)
XLA Modules:
  0.0 32.8 jit_solution(1109683667896316144)
XLA Ops:
  0.0 30.7 %gather_pairs.1 = (bf16[512,1024]{1,0:T(8,128)(2,1)S(1)}, bf16[512,1024]{1,0:T(8,128)(2,1)S(1)}, f32[1024,1024]{1,0:T(8,128)S(1)}) custom-call(bf16[16,1024]{1,0:T(8,128)(2,1)} %bitcast.3, bf16[16,1024]{1,0:T(8,128)(2,1)} %amp_in.1, f32[1,128]{1,0:T(1,128)} %bitcast.4, f32[1,128]{1,0:T(1,128)} %bitcast.5), custom_call_target="tpu_custom_call" | custom-call | tf_op jit(solution)/shard_map/gather_pairs/pallas_call | solution.py:221
  30.7 2.1 %ladder_sum.1 = bf16[1024,1024]{1,0:T(8,128)(2,1)} custom-call(bf16[512,1024]{1,0:T(8,128)(2,1)S(1)} %get-tuple-element.8.int_ref, bf16[512,1024]{1,0:T(8,128)(2,1)S(1)} %get-tuple-element.9.amp_ref, f32[1024,1024]{1,0:T(8,128)S(1)} %get-tuple-element.10.inverse), custom_call_target="tpu_custom_call" | custom-call | tf_op jit(solution)/shard_map/ladder_sum/pallas_call | solution.py:259

commit v4 on v3

--- a/solution.py
+++ b/solution.py
@@ -23,10 +23,25 @@
     return pl.ds(pl.multiple_of(kind * CD + owner * CDS, CDS), CDS)
 
 
-def split_by_partner(chunk, turn, pieces):
+def split_by_partner(chunk, turn):
     for j in range(OWN):
         turn[pl.ds(j, CDS, stride=OWN), :] = chunk[:, j * ORB : (j + 1) * ORB].astype(jnp.float32)
-    pieces[...] = turn[...].T.reshape(pieces.shape)
+    turned = turn[...].T
+    return [turned[p * OWN : (p + 1) * OWN] for p in range(GROUP)]
+
+
+def swap_order(rows):
+    return [rows[(p % RING) * RING + p // RING] for p in range(GROUP)]
+
+
+def put_rows(rows, held):
+    for q in range(RING):
+        held[q] = jnp.concatenate(rows[q * RING : (q + 1) * RING], axis=0).astype(held.dtype)
+
+
+def take_rows(held):
+    blocks = [held[q].astype(jnp.float32) for q in range(RING)]
+    return [blocks[p // RING][(p % RING) * OWN : (p % RING + 1) * OWN] for p in range(GROUP)]
 
 
 def join_from_partners(rows, turn, chunk):
@@ -46,7 +61,7 @@
 
 def gather_kernel(
     int_in, amp_in, occ_in, vir_in, int_all, amp_all, inverse,
-    int_cut, int_got, amp_cut, amp_x, amp_z, turn,
+    int_cut, int_got, amp_cut, amp_z, amp_cut_x, amp_x, turn,
     occ_row, vir_row, occ_at, vir_at,
     local_sem, pair_send, pair_recv, int_send, int_recv, amp_send, amp_recv,
 ):
@@ -66,17 +81,18 @@
     def at_chip(y_step, other):
         return (around(y, y_step) * 4 + (1 - z_lo if other else z_lo) * 2 + core, oo)
 
-    def at_vv(step):
-        return (lax.rem(vv + step, GROUP), oo)
+    def at_vv(y_step, other, twin):
+        return around(y, y_step) * 4 + (1 - z_lo if other else z_lo) * 2 + (1 - core if twin else core)
 
     sibling = (y * 4 + z_lo * 2 + 1 - core, oo)
-    near = (1, -1, 2)
+    near, far_first = (1, -1, 2), (2, 1, -1)
+    x_steps = ((1, -1), far_first)
+    rows_of = [
+        (y_step, other, twin)
+        for y_step in (*far_first, 0) for other in (True, False) for twin in (True, False)
+    ][:-1]
     chips = [(step, other) for other in (False, True) for step in (0, *near) if step != 0 or other]
 
-    barrier = pltpu.get_barrier_semaphore()
-    greeted = [at_z(step) for step in near] + [at_x(step) for step in near] + [at_vv(step) for step in range(1, GROUP)]
-    for device in greeted:
-        pl.semaphore_signal(barrier, inc=1, device_id=device, device_id_type=MESH)
     loads = [
         pltpu.make_async_copy(int_in, int_all.at[slot(0, oo)], local_sem.at[0]),
         pltpu.make_async_copy(amp_in, amp_all.at[slot(0, vv)], local_sem.at[1]),
@@ -87,11 +103,16 @@
     ]
     for load in loads:
         load.start()
-    for load in loads:
+    barrier = pltpu.get_barrier_semaphore()
+    greeted = [at_z(step) for step in far_first] + [(at_vv(*steps), oo) for steps in rows_of] + [at_x(step) for step in far_first]
+    for device in greeted:
+        pl.semaphore_signal(barrier, inc=1, device_id=device, device_id_type=MESH)
+    for load in loads[:2]:
         load.wait()
 
-    split_by_partner(amp_all.at[slot(0, vv)], turn.at[1], amp_cut)
-    split_by_partner(int_all.at[slot(0, oo)], turn.at[0], int_cut)
+    put_rows(swap_order(split_by_partner(amp_all.at[slot(0, vv)], turn.at[1])), amp_cut)
+    for p, row in enumerate(split_by_partner(int_all.at[slot(0, oo)], turn.at[0])):
+        int_cut[p] = row
     pl.semaphore_wait(barrier, len(greeted))
 
     sent = []
@@ -130,6 +151,68 @@
     def got_amp(kind, owner):
         got(amp_all.at[slot(kind, owner)], amp_recv.at[kind, owner])
 
+    def spread_int(kind):
+        for step in far_first:
+            send_int(kind, oo, at_z(step))
+        for step in (1, -1):
+            send_int(kind, oo, at_x(step))
+
+    def spread_amp(kind):
+        for step, other in chips:
+            send_amp(kind, vv, at_chip(step, other))
+        send_amp(kind, vv, sibling)
+
+    def owner_int(x_step, z_step):
+        return around(x, x_step) * 4 + around(z_hi, z_step)
+
+    def owner_amp(y_step, other):
+        return around(y, y_step) * 4 + (1 - z_lo if other else z_lo) * 2 + core
+
+    def onward_int(kind):
+        for z_step in near:
+            got_int(kind, owner_int(0, z_step))
+            for step in x_steps[kind]:
+                send_int(kind, owner_int(0, z_step), at_x(step))
+
+    def relay_int(kind, z_step):
+        first = -1 if z_step % 2 == 0 else 1
+        got_int(kind, owner_int(first, z_step))
+        send_int(kind, owner_int(first, z_step), at_x(-first))
+
+    def onward_amp(kind):
+        for step, other in chips:
+            got_amp(kind, owner_amp(step, other))
+            send_amp(kind, owner_amp(step, other), sibling)
+
+    def spread_direct():
+        send_amp(0, vv, at_chip(0, True))
+        for step in far_first:
+            send_amp(0, vv, at_chip(step, False))
+        send_amp(0, vv, sibling)
+
+    def onward_direct():
+        got_amp(0, owner_amp(0, True))
+        for step in far_first:
+            send_amp(0, owner_amp(0, True), at_chip(step, False))
+        send_amp(0, owner_amp(0, True), sibling)
+
+    def pass_direct():
+        for other in (False, True):
+            for step in near:
+                got_amp(0, owner_amp(step, other))
+                send_amp(0, owner_amp(step, other), sibling)
+
+    for step in far_first:
+        send_pair(amp_cut.at[around(z_hi, step)], amp_z.at[z_hi], step % RING, at_z(step))
+    for n, steps in enumerate(rows_of):
+        partner = at_vv(*steps)
+        send_pair(int_cut.at[partner], int_got.at[vv], 8 + n, (partner, oo))
+    amp_z[z_hi] = amp_cut[z_hi]
+    int_got[vv] = int_cut[vv]
+    spread_int(0)
+    spread_direct()
+    for load in loads[2:]:
+        load.wait()
     vir_column = jnp.broadcast_to(vir_row[...], (ORB, ORB)).T
 
     def invert(blocks):
@@ -139,69 +222,43 @@
                 denom = (occ_at[0, oo * OWN + i] + occ_row[...]) - vir_pair
                 inverse[a * ORB : (a + 1) * ORB, i * ORB : (i + 1) * ORB] = 1.0 / denom
 
-    def spread_int(kind):
-        for step in near:
-            send_int(kind, oo, at_z(step))
-        for step in near:
-            send_int(kind, oo, at_x(step))
-
-    def spread_amp(kind):
-        for step, other in chips:
-            send_amp(kind, vv, at_chip(step, other))
-        send_amp(kind, vv, sibling)
-
-    def owner_int(x_step, z_step):
-        return around(x, x_step) * 4 + around(z_hi, z_step)
-
-    def owner_amp(y_step, other):
-        return around(y, y_step) * 4 + (1 - z_lo if other else z_lo) * 2 + core
-
-    def onward_int(kind):
-        for z_step in near:
-            got_int(kind, owner_int(0, z_step))
-            for step in near:
-                send_int(kind, owner_int(0, z_step), at_x(step))
-
-    def onward_amp(kind):
-        for step, other in chips:
-            got_amp(kind, owner_amp(step, other))
-            send_amp(kind, owner_amp(step, other), sibling)
+    invert(range(0, 2))
+
+    for n, (y_step, other, twin) in enumerate(rows_of):
+        back = y_step if y_step == 2 else -y_step
+        got(int_got.at[at_vv(back, other, twin)], pair_recv.at[8 + n])
 
     for step in near:
-        send_pair(amp_cut.at[around(x, step)], amp_x.at[x], step % RING, at_x(step))
-    for step in range(1, GROUP):
-        send_pair(int_cut.at[lax.rem(vv + step, GROUP)], int_got.at[vv], 8 + step, at_vv(step))
-    amp_x[x] = amp_cut[x]
-    int_got[vv] = int_cut[vv]
-    spread_int(0)
-    spread_amp(0)
-    invert(range(0, 2))
-
-    for step in near:
-        got(amp_x.at[around(x, step)], pair_recv.at[-step % RING])
-    for step in near:
-        send_pair(amp_x.at[:, around(z_hi, step)], amp_z.at[:, z_hi], 4 + step % RING, at_z(step))
-    amp_z[:, z_hi] = amp_x[:, z_hi]
-
-    for step in range(1, GROUP):
-        got(int_got.at[lax.rem(vv + GROUP - step, GROUP)], pair_recv.at[8 + step])
+        got(amp_z.at[around(z_hi, step)], pair_recv.at[-step % RING])
+    put_rows(swap_order(take_rows(amp_z)), amp_cut_x)
+    for step in far_first:
+        send_pair(amp_cut_x.at[around(x, step)], amp_x.at[x], 4 + step % RING, at_x(step))
+    amp_x[x] = amp_cut_x[x]
     join_from_partners([int_got[p] for p in range(GROUP)], turn.at[0], int_all.at[slot(1, oo)])
     spread_int(1)
+
+    onward_direct()
     invert(range(2, 3))
     onward_int(0)
+    relay_int(0, 0)
 
     for step in near:
-        got(amp_z.at[:, around(z_hi, step)], pair_recv.at[4 + -step % RING])
-    join_from_partners([amp_z[p // 4, p % 4] for p in range(GROUP)], turn.at[1], amp_all.at[slot(1, vv)])
+        got(amp_x.at[around(x, step)], pair_recv.at[4 + -step % RING])
+    join_from_partners(take_rows(amp_x), turn.at[1], amp_all.at[slot(1, vv)])
     spread_amp(1)
-    onward_amp(0)
+    relay_int(0, 1)
+    relay_int(0, -1)
+    pass_direct()
+    relay_int(0, 2)
+    relay_int(1, 0)
     onward_int(1)
     invert(range(3, 8))
     onward_amp(1)
     for kind in range(2):
-        for step in near:
-            for z_step in range(4):
-                got_int(kind, owner_int(step, z_step))
+        for z_step in (0, 1, -1, 2):
+            for step in near:
+                if (kind == 1 and z_step != 0) or step != (-1 if z_step % 2 == 0 else 1):
+                    got_int(kind, owner_int(step, z_step))
         for far in range(8):
             got_amp(kind, far * 2 + 1 - core)
     for copy in sent:
@@ -213,6 +270,8 @@
 
     def pieces(*shape):
         return pltpu.VMEM((*shape, OWN, ORB), jnp.float32)
+
+    blocks = pltpu.VMEM((RING, RING * OWN, ORB), jnp.bfloat16)
 
     def dma(*shape):
         return pltpu.SemaphoreType.DMA(shape)
@@ -224,7 +283,7 @@
         in_specs=[pl.BlockSpec(memory_space=pltpu.HBM)] * 4,
         out_specs=(pl.BlockSpec(memory_space=pltpu.VMEM),) * 3,
         scratch_shapes=[
-            pieces(GROUP), pieces(GROUP), pieces(4, 4), pieces(4, 4), pieces(4, 4),
+            pieces(GROUP), pieces(GROUP), blocks, blocks, blocks, blocks,
             pltpu.VMEM((2, ORB, ORB), jnp.float32),
             pltpu.VMEM((1, ORB), jnp.float32), pltpu.VMEM((1, ORB), jnp.float32),
             pltpu.SMEM((1, ORB), jnp.float32), pltpu.SMEM((1, ORB), jnp.float32),

time: 33 us -> 30.7 us (0.930)
  the two profiles are of different devices: /device:TPU:1 before, /device:TPU:2 now
where the time goes in v4:
time: 30.7 us; the launch traced here: 30.6 us
  Pallas kernels  30.6 us (100%)
    pallas_call x1, Pallas kernels, gathered(): pl.pallas_call(gather_kernel, out_shape=(whole, whole, pltpu.VMEM((WIDE,...  28.5 us
    pallas_call x1, Pallas kernels, ladder(): pl.pallas_call(ladder_kernel, out_shape=jax.ShapeDtypeStruct((WIDE, WIDE)...  2.12 us

profile of v4, /device:TPU:2, one launch (start us, length us, event | category | flops | bytes accessed | tf_op | source)
XLA Modules:
  0.0 30.6 jit_solution(11781381568277558608)
XLA Ops:
  0.0 28.5 %gather_pairs.1 = (bf16[512,1024]{1,0:T(8,128)(2,1)S(1)}, bf16[512,1024]{1,0:T(8,128)(2,1)S(1)}, f32[1024,1024]{1,0:T(8,128)S(1)}) custom-call(bf16[16,1024]{1,0:T(8,128)(2,1)} %bitcast.3, bf16[16,1024]{1,0:T(8,128)(2,1)} %amp_in.1, f32[1,128]{1,0:T(1,128)} %bitcast.4, f32[1,128]{1,0:T(1,128)} %bitcast.5), custom_call_target="tpu_custom_call" | custom-call | tf_op jit(solution)/shard_map/gather_pairs/pallas_call | solution.py:280
  28.5 2.1 %ladder_sum.1 = bf16[1024,1024]{1,0:T(8,128)(2,1)} custom-call(bf16[512,1024]{1,0:T(8,128)(2,1)S(1)} %get-tuple-element.8.int_ref, bf16[512,1024]{1,0:T(8,128)(2,1)S(1)} %get-tuple-element.9.amp_ref, f32[1024,1024]{1,0:T(8,128)S(1)} %get-tuple-element.10.inverse), custom_call_target="tpu_custom_call" | custom-call | tf_op jit(solution)/shard_map/ladder_sum/pallas_call | solution.py:318

commit v5 on v4

--- a/solution.py
+++ b/solution.py
@@ -13,6 +13,7 @@
 WIDE = OWN * ORB
 CD = GROUP * CDS
 RING = 4
+ROWS = 256
 
 
 def around(at, step):
@@ -60,7 +61,7 @@
 
 
 def gather_kernel(
-    int_in, amp_in, occ_in, vir_in, int_all, amp_all, inverse,
+    int_in, amp_in, occ_in, vir_in, int_all, amp_all, inverse, partial,
     int_cut, int_got, amp_cut, amp_z, amp_cut_x, amp_x, turn,
     occ_row, vir_row, occ_at, vir_at,
     local_sem, pair_send, pair_recv, int_send, int_recv, amp_send, amp_recv,
@@ -91,8 +92,12 @@
         (y_step, other, twin)
         for y_step in (*far_first, 0) for other in (True, False) for twin in (True, False)
     ][:-1]
-    chips = [(step, other) for other in (False, True) for step in (0, *near) if step != 0 or other]
-
+    chips = [
+        (1, False), (-1, False), (0, True), (2, False), (1, True), (-1, True), (2, True)
+    ]
+
+    barrier = pltpu.get_barrier_semaphore()
+    greeted = [at_z(step) for step in far_first] + [(at_vv(*steps), oo) for steps in rows_of] + [at_x(step) for step in far_first]
     loads = [
         pltpu.make_async_copy(int_in, int_all.at[slot(0, oo)], local_sem.at[0]),
         pltpu.make_async_copy(amp_in, amp_all.at[slot(0, vv)], local_sem.at[1]),
@@ -101,16 +106,16 @@
         pltpu.make_async_copy(occ_in, occ_at, local_sem.at[4]),
         pltpu.make_async_copy(vir_in, vir_at, local_sem.at[5]),
     ]
-    for load in loads:
+    for n, device in enumerate(greeted):
+        if n in (1, 2):
+            loads[2 - n].start()
+        pl.semaphore_signal(barrier, inc=1, device_id=device, device_id_type=MESH)
+    for load in loads[2:]:
         load.start()
-    barrier = pltpu.get_barrier_semaphore()
-    greeted = [at_z(step) for step in far_first] + [(at_vv(*steps), oo) for steps in rows_of] + [at_x(step) for step in far_first]
-    for device in greeted:
-        pl.semaphore_signal(barrier, inc=1, device_id=device, device_id_type=MESH)
-    for load in loads[:2]:
-        load.wait()
-
+
+    loads[1].wait()
     put_rows(swap_order(split_by_partner(amp_all.at[slot(0, vv)], turn.at[1])), amp_cut)
+    loads[0].wait()
     for p, row in enumerate(split_by_partner(int_all.at[slot(0, oo)], turn.at[0])):
         int_cut[p] = row
     pl.semaphore_wait(barrier, len(greeted))
@@ -158,7 +163,7 @@
             send_int(kind, oo, at_x(step))
 
     def spread_amp(kind):
-        for step, other in chips:
+        for step, other in chips[::-1]:
             send_amp(kind, vv, at_chip(step, other))
         send_amp(kind, vv, sibling)
 
@@ -168,8 +173,8 @@
     def owner_amp(y_step, other):
         return around(y, y_step) * 4 + (1 - z_lo if other else z_lo) * 2 + core
 
-    def onward_int(kind):
-        for z_step in near:
+    def onward_int(kind, z_steps=near):
+        for z_step in z_steps:
             got_int(kind, owner_int(0, z_step))
             for step in x_steps[kind]:
                 send_int(kind, owner_int(0, z_step), at_x(step))
@@ -248,25 +253,36 @@
     spread_amp(1)
     relay_int(0, 1)
     relay_int(0, -1)
+    relay_int(1, 0)
+    onward_int(1, (1, -1))
+    relay_int(0, 2)
+    onward_int(1, (2,))
     pass_direct()
-    relay_int(0, 2)
-    relay_int(1, 0)
-    onward_int(1)
     invert(range(3, 8))
     onward_amp(1)
-    for kind in range(2):
+    def finish(kind):
         for z_step in (0, 1, -1, 2):
             for step in near:
                 if (kind == 1 and z_step != 0) or step != (-1 if z_step % 2 == 0 else 1):
                     got_int(kind, owner_int(step, z_step))
         for far in range(8):
             got_amp(kind, far * 2 + 1 - core)
+
+    finish(0)
+    for at in range(0, WIDE, ROWS):
+        partial[at : at + ROWS] = lax.dot_general(
+            int_all[:CD, at : at + ROWS], amp_all[:CD], (((0,), (0,)), ((), ())),
+            preferred_element_type=jnp.float32,
+        )
+    finish(1)
     for copy in sent:
         copy.wait_send()
 
 
 def gathered(integrals_t, amplitudes, occ_row, vir_row):
     whole = pltpu.VMEM((2 * CD, WIDE), jnp.bfloat16)
+
+    square = pltpu.VMEM((WIDE, WIDE), jnp.float32)
 
     def pieces(*shape):
         return pltpu.VMEM((*shape, OWN, ORB), jnp.float32)
@@ -279,9 +295,9 @@
     held = [pltpu.with_memory_space_constraint(a, pltpu.HBM) for a in (integrals_t, amplitudes, occ_row, vir_row)]
     return pl.pallas_call(
         gather_kernel,
-        out_shape=(whole, whole, pltpu.VMEM((WIDE, WIDE), jnp.float32)),
+        out_shape=(whole, whole, square, square),
         in_specs=[pl.BlockSpec(memory_space=pltpu.HBM)] * 4,
-        out_specs=(pl.BlockSpec(memory_space=pltpu.VMEM),) * 3,
+        out_specs=(pl.BlockSpec(memory_space=pltpu.VMEM),) * 4,
         scratch_shapes=[
             pieces(GROUP), pieces(GROUP), blocks, blocks, blocks, blocks,
             pltpu.VMEM((2, ORB, ORB), jnp.float32),
@@ -296,36 +312,33 @@
     )(*held)
 
 
-ROWS = 256
-
-
-def ladder_kernel(int_ref, amp_ref, inverse, out_ref, made, sems):
+def ladder_kernel(int_ref, amp_ref, inverse, partial, out_ref, made, sems):
     copies = []
     for s in range(WIDE // ROWS):
         rows = pl.ds(s * ROWS, ROWS)
         total = lax.dot_general(
-            int_ref[:, s * ROWS : (s + 1) * ROWS], amp_ref[...], (((0,), (0,)), ((), ())),
+            int_ref[CD:, s * ROWS : (s + 1) * ROWS], amp_ref[CD:], (((0,), (0,)), ((), ())),
             preferred_element_type=jnp.float32,
         )
-        made[rows, :] = (total * inverse[rows, :]).astype(made.dtype)
+        made[rows, :] = ((partial[rows, :] + total) * inverse[rows, :]).astype(made.dtype)
         copies.append(pltpu.make_async_copy(made.at[rows], out_ref.at[rows], sems.at[s]))
         copies[-1].start()
     for copy in copies:
         copy.wait()
 
 
-def ladder(int_all, amp_all, inverse):
+def ladder(int_all, amp_all, inverse, partial):
     return pl.pallas_call(
         ladder_kernel,
         out_shape=jax.ShapeDtypeStruct((WIDE, WIDE), jnp.bfloat16),
-        in_specs=[pl.BlockSpec(memory_space=pltpu.VMEM)] * 3,
+        in_specs=[pl.BlockSpec(memory_space=pltpu.VMEM)] * 4,
         out_specs=pl.BlockSpec(memory_space=pl.ANY),
         scratch_shapes=[
             pltpu.VMEM((WIDE, WIDE), jnp.bfloat16), pltpu.SemaphoreType.DMA((WIDE // ROWS,)),
         ],
         compiler_params=pltpu.CompilerParams(vmem_limit_bytes=32 << 20),
         name="ladder_sum",
-    )(int_all, amp_all, inverse)
+    )(int_all, amp_all, inverse, partial)
 
 
 def on_device(integrals, amplitudes, occ_energy, vir_energy):

time: 30.7 us -> 29.6 us (0.964)
  the two profiles are of different devices: /device:TPU:2 before, /device:TPU:1 now
where the time goes in v5:
time: 29.6 us; the launch traced here: 29.3 us
  Pallas kernels  29.3 us (99%)
    pallas_call x1, Pallas kernels, gathered(): pl.pallas_call(gather_kernel, out_shape=(whole, whole, square, square), i...  27.6 us
    pallas_call x1, Pallas kernels, ladder(): pl.pallas_call(ladder_kernel, out_shape=jax.ShapeDtypeStruct((WIDE, WIDE)...  1.7 us

profile of v5, /device:TPU:1, one launch (start us, length us, event | category | flops | bytes accessed | tf_op | source)
XLA Modules:
  0.0 29.3 jit_solution(10903328984355788304)
XLA Ops:
  0.0 27.6 %gather_pairs.1 = (bf16[512,1024]{1,0:T(8,128)(2,1)S(1)}, bf16[512,1024]{1,0:T(8,128)(2,1)S(1)}, f32[1024,1024]{1,0:T(8,128)S(1)}, f32[1024,1024]{1,0:T(8,128)S(1)}) custom-call(bf16[16,1024]{1,0:T(8,128)(2,1)} %bitcast.3, bf16[16,1024]{1,0:T(8,128)(2,1)} %amp_in.1, f32[1,128]{1,0:T(1,128)} %bitcast.4, f32[1,128]{1,0:T(1,128)} %bitcast.5), custom_call_target="tpu_custom_call" | custom-call | tf_op jit(solution)/shard_map/gather_pairs/pallas_call | solution.py:296
  27.6 1.7 %ladder_sum.1 = bf16[1024,1024]{1,0:T(8,128)(2,1)} custom-call(bf16[512,1024]{1,0:T(8,128)(2,1)S(1)} %get-tuple-element.9.int_ref, bf16[512,1024]{1,0:T(8,128)(2,1)S(1)} %get-tuple-element.10.amp_ref, f32[1024,1024]{1,0:T(8,128)S(1)} %get-tuple-element.11.inverse, f32[1024,1024]{1,0:T(8,128)S(1)} %get-tuple-element.12.partial), custom_call_target="tpu_custom_call" | custom-call | tf_op jit(solution)/shard_map/ladder_sum/pallas_call | solution.py:331

commit v6 on v5

--- a/solution.py
+++ b/solution.py
@@ -64,7 +64,7 @@
     int_in, amp_in, occ_in, vir_in, int_all, amp_all, inverse, partial,
     int_cut, int_got, amp_cut, amp_z, amp_cut_x, amp_x, turn,
     occ_row, vir_row, occ_at, vir_at,
-    local_sem, pair_send, pair_recv, int_send, int_recv, amp_send, amp_recv,
+    local_sem, pair_send, pair_recv, int_send, int_recv, int_done, amp_send, amp_recv, amp_done,
 ):
     vv, oo = lax.axis_index("vv"), lax.axis_index("oo")
     y, z_lo, core = vv // 4, (vv // 2) % 2, vv % 2
@@ -120,32 +120,29 @@
         int_cut[p] = row
     pl.semaphore_wait(barrier, len(greeted))
 
-    sent = []
-
     def send(src, dst, send_sem, recv_sem, device):
         copy = pltpu.make_async_remote_copy(
             src_ref=src, dst_ref=dst, send_sem=send_sem, recv_sem=recv_sem,
             device_id=device, device_id_type=MESH,
         )
         copy.start()
-        sent.append(copy)
-
-    used = {"int": 0, "amp": 0, "pair": 0}
-
-    def next_of(which):
-        used[which] += 1
-        return used[which] - 1
-
-    def send_int(kind, owner, device):
+
+    used = {"int": 0, "amp": 0}
+
+    def send_int(kind, owner, device, last=False):
         rows = int_all.at[slot(kind, owner)]
-        send(rows, rows, int_send.at[next_of("int")], int_recv.at[kind, owner], device)
-
-    def send_amp(kind, owner, device):
+        used["int"] += 1
+        arrival = int_done.at[kind] if last else int_recv.at[kind, owner]
+        send(rows, rows, int_send.at[0], arrival, device)
+
+    def send_amp(kind, owner, device, last=False):
         rows = amp_all.at[slot(kind, owner)]
-        send(rows, rows, amp_send.at[next_of("amp")], amp_recv.at[kind, owner], device)
-
-    def send_pair(src, dst, arrival, device):
-        send(src, dst, pair_send.at[next_of("pair")], pair_recv.at[arrival], device)
+        used["amp"] += 1
+        arrival = amp_done.at[kind] if last else amp_recv.at[kind, owner]
+        send(rows, rows, amp_send.at[0], arrival, device)
+
+    def send_pair(which, src, dst, arrival, device):
+        send(src, dst, pair_send.at[which], pair_recv.at[arrival], device)
 
     def got(ref, sem):
         pltpu.make_async_copy(ref, ref, sem).wait()
@@ -160,12 +157,12 @@
         for step in far_first:
             send_int(kind, oo, at_z(step))
         for step in (1, -1):
-            send_int(kind, oo, at_x(step))
+            send_int(kind, oo, at_x(step), last=step == -1)
 
     def spread_amp(kind):
         for step, other in chips[::-1]:
             send_amp(kind, vv, at_chip(step, other))
-        send_amp(kind, vv, sibling)
+        send_amp(kind, vv, sibling, last=True)
 
     def owner_int(x_step, z_step):
         return around(x, x_step) * 4 + around(z_hi, z_step)
@@ -177,41 +174,42 @@
         for z_step in z_steps:
             got_int(kind, owner_int(0, z_step))
             for step in x_steps[kind]:
-                send_int(kind, owner_int(0, z_step), at_x(step))
+                last = kind == 1 or step != (1 if z_step % 2 == 0 else -1)
+                send_int(kind, owner_int(0, z_step), at_x(step), last)
 
     def relay_int(kind, z_step):
         first = -1 if z_step % 2 == 0 else 1
         got_int(kind, owner_int(first, z_step))
-        send_int(kind, owner_int(first, z_step), at_x(-first))
+        send_int(kind, owner_int(first, z_step), at_x(-first), last=True)
 
     def onward_amp(kind):
         for step, other in chips:
             got_amp(kind, owner_amp(step, other))
-            send_amp(kind, owner_amp(step, other), sibling)
+            send_amp(kind, owner_amp(step, other), sibling, last=True)
 
     def spread_direct():
         send_amp(0, vv, at_chip(0, True))
         for step in far_first:
             send_amp(0, vv, at_chip(step, False))
-        send_amp(0, vv, sibling)
+        send_amp(0, vv, sibling, last=True)
 
     def onward_direct():
         got_amp(0, owner_amp(0, True))
         for step in far_first:
             send_amp(0, owner_amp(0, True), at_chip(step, False))
-        send_amp(0, owner_amp(0, True), sibling)
+        send_amp(0, owner_amp(0, True), sibling, last=True)
 
     def pass_direct():
         for other in (False, True):
             for step in near:
                 got_amp(0, owner_amp(step, other))
-                send_amp(0, owner_amp(step, other), sibling)
+                send_amp(0, owner_amp(step, other), sibling, last=True)
 
     for step in far_first:
-        send_pair(amp_cut.at[around(z_hi, step)], amp_z.at[z_hi], step % RING, at_z(step))
-    for n, steps in enumerate(rows_of):
+        send_pair(0, amp_cut.at[around(z_hi, step)], amp_z.at[z_hi], step % RING, at_z(step))
+    for steps in rows_of:
         partner = at_vv(*steps)
-        send_pair(int_cut.at[partner], int_got.at[vv], 8 + n, (partner, oo))
+        send_pair(2, int_cut.at[partner], int_got.at[vv], 8, (partner, oo))
     amp_z[z_hi] = amp_cut[z_hi]
     int_got[vv] = int_cut[vv]
     spread_int(0)
@@ -227,23 +225,21 @@
                 denom = (occ_at[0, oo * OWN + i] + occ_row[...]) - vir_pair
                 inverse[a * ORB : (a + 1) * ORB, i * ORB : (i + 1) * ORB] = 1.0 / denom
 
-    invert(range(0, 2))
-
-    for n, (y_step, other, twin) in enumerate(rows_of):
-        back = y_step if y_step == 2 else -y_step
-        got(int_got.at[at_vv(back, other, twin)], pair_recv.at[8 + n])
+    invert(range(0, 6))
+
+    got(int_got.at[pl.ds(0, GROUP - 1)], pair_recv.at[8])
 
     for step in near:
         got(amp_z.at[around(z_hi, step)], pair_recv.at[-step % RING])
     put_rows(swap_order(take_rows(amp_z)), amp_cut_x)
     for step in far_first:
-        send_pair(amp_cut_x.at[around(x, step)], amp_x.at[x], 4 + step % RING, at_x(step))
+        send_pair(1, amp_cut_x.at[around(x, step)], amp_x.at[x], 4 + step % RING, at_x(step))
     amp_x[x] = amp_cut_x[x]
     join_from_partners([int_got[p] for p in range(GROUP)], turn.at[0], int_all.at[slot(1, oo)])
     spread_int(1)
 
     onward_direct()
-    invert(range(2, 3))
+    invert(range(6, 8))
     onward_int(0)
     relay_int(0, 0)
 
@@ -258,15 +254,10 @@
     relay_int(0, 2)
     onward_int(1, (2,))
     pass_direct()
-    invert(range(3, 8))
     onward_amp(1)
     def finish(kind):
-        for z_step in (0, 1, -1, 2):
-            for step in near:
-                if (kind == 1 and z_step != 0) or step != (-1 if z_step % 2 == 0 else 1):
-                    got_int(kind, owner_int(step, z_step))
-        for far in range(8):
-            got_amp(kind, far * 2 + 1 - core)
+        got(int_all.at[pl.ds(0, (8 if kind == 0 else 11) * CDS)], int_done.at[kind])
+        got(amp_all.at[pl.ds(0, 8 * CDS)], amp_done.at[kind])
 
     finish(0)
     for at in range(0, WIDE, ROWS):
@@ -275,8 +266,11 @@
             preferred_element_type=jnp.float32,
         )
     finish(1)
-    for copy in sent:
-        copy.wait_send()
+    got(amp_cut.at[pl.ds(0, RING - 1)], pair_send.at[0])
+    got(amp_cut_x.at[pl.ds(0, RING - 1)], pair_send.at[1])
+    got(int_cut.at[pl.ds(0, GROUP - 1)], pair_send.at[2])
+    got(int_all.at[pl.ds(0, used["int"] * CDS)], int_send.at[0])
+    got(amp_all.at[pl.ds(0, used["amp"] * CDS)], amp_send.at[0])
 
 
 def gathered(integrals_t, amplitudes, occ_row, vir_row):
@@ -303,7 +297,7 @@
             pltpu.VMEM((2, ORB, ORB), jnp.float32),
             pltpu.VMEM((1, ORB), jnp.float32), pltpu.VMEM((1, ORB), jnp.float32),
             pltpu.SMEM((1, ORB), jnp.float32), pltpu.SMEM((1, ORB), jnp.float32),
-            dma(6), dma(21), dma(8 + GROUP), dma(30), dma(2, GROUP), dma(30), dma(2, GROUP),
+            dma(6), dma(3), dma(9), dma(1), dma(2, GROUP), dma(2), dma(1), dma(2, GROUP), dma(2),
         ],
         compiler_params=pltpu.CompilerParams(
             collective_id=0, has_side_effects=True, vmem_limit_bytes=32 << 20

time: 29.6 us -> 28.6 us (0.966)
  Pallas kernels: 29.3 us -> 28.4 us
    pallas_call x1, Pallas kernels: 27.6 us -> 26.7 us  [gathered(): pl.pallas_call(gather_kernel, out_shape=(whole, whole, square, square), i...]
where the time goes in v6:
time: 28.6 us; the launch traced here: 28.4 us
  Pallas kernels  28.4 us (99%)
    pallas_call x1, Pallas kernels, gathered(): pl.pallas_call(gather_kernel, out_shape=(whole, whole, square, square), i...  26.7 us
    pallas_call x1, Pallas kernels, ladder(): pl.pallas_call(ladder_kernel, out_shape=jax.ShapeDtypeStruct((WIDE, WIDE)...  1.68 us

profile of v6, /device:TPU:1, one launch (start us, length us, event | category | flops | bytes accessed | tf_op | source)
XLA Modules:
  0.0 28.4 jit_solution(6913641464339274266)
XLA Ops:
  0.0 26.7 %gather_pairs.1 = (bf16[512,1024]{1,0:T(8,128)(2,1)S(1)}, bf16[512,1024]{1,0:T(8,128)(2,1)S(1)}, f32[1024,1024]{1,0:T(8,128)S(1)}, f32[1024,1024]{1,0:T(8,128)S(1)}) custom-call(bf16[16,1024]{1,0:T(8,128)(2,1)} %bitcast.3, bf16[16,1024]{1,0:T(8,128)(2,1)} %amp_in.1, f32[1,128]{1,0:T(1,128)} %bitcast.4, f32[1,128]{1,0:T(1,128)} %bitcast.5), custom_call_target="tpu_custom_call" | custom-call | tf_op jit(solution)/shard_map/gather_pairs/pallas_call | solution.py:290
  26.7 1.7 %ladder_sum.1 = bf16[1024,1024]{1,0:T(8,128)(2,1)} custom-call(bf16[512,1024]{1,0:T(8,128)(2,1)S(1)} %get-tuple-element.9.int_ref, bf16[512,1024]{1,0:T(8,128)(2,1)S(1)} %get-tuple-element.10.amp_ref, f32[1024,1024]{1,0:T(8,128)S(1)} %get-tuple-element.11.inverse, f32[1024,1024]{1,0:T(8,128)S(1)} %get-tuple-element.12.partial), custom_call_target="tpu_custom_call" | custom-call | tf_op jit(solution)/shard_map/ladder_sum/pallas_call | solution.py:325

commit v7 on v6

--- a/solution.py
+++ b/solution.py
@@ -87,7 +87,6 @@
 
     sibling = (y * 4 + z_lo * 2 + 1 - core, oo)
     near, far_first = (1, -1, 2), (2, 1, -1)
-    x_steps = ((1, -1), far_first)
     rows_of = [
         (y_step, other, twin)
         for y_step in (*far_first, 0) for other in (True, False) for twin in (True, False)
@@ -156,8 +155,8 @@
     def spread_int(kind):
         for step in far_first:
             send_int(kind, oo, at_z(step))
-        for step in (1, -1):
-            send_int(kind, oo, at_x(step), last=step == -1)
+        for step in (1, -1) if kind == 0 else far_first:
+            send_int(kind, oo, at_x(step), last=step == -1 or (kind == 1 and step == 1))
 
     def spread_amp(kind):
         for step, other in chips[::-1]:
@@ -173,9 +172,15 @@
     def onward_int(kind, z_steps=near):
         for z_step in z_steps:
             got_int(kind, owner_int(0, z_step))
-            for step in x_steps[kind]:
-                last = kind == 1 or step != (1 if z_step % 2 == 0 else -1)
+            relayed = kind == 0 and z_step != 2
+            for step in far_first if z_step == 2 else (1, -1):
+                last = not relayed or step != (1 if z_step % 2 == 0 else -1)
                 send_int(kind, owner_int(0, z_step), at_x(step), last)
+
+    def corner_int():
+        got_int(1, owner_int(2, 0))
+        for step in (1, -1):
+            send_int(1, owner_int(2, 0), at_z(step), last=True)
 
     def relay_int(kind, z_step):
         first = -1 if z_step % 2 == 0 else 1
@@ -206,7 +211,7 @@
                 send_amp(0, owner_amp(step, other), sibling, last=True)
 
     for step in far_first:
-        send_pair(0, amp_cut.at[around(z_hi, step)], amp_z.at[z_hi], step % RING, at_z(step))
+        send_pair(0, amp_cut.at[around(z_hi, step)], amp_z.at[z_hi], 0, at_z(step))
     for steps in rows_of:
         partner = at_vv(*steps)
         send_pair(2, int_cut.at[partner], int_got.at[vv], 8, (partner, oo))
@@ -229,11 +234,10 @@
 
     got(int_got.at[pl.ds(0, GROUP - 1)], pair_recv.at[8])
 
-    for step in near:
-        got(amp_z.at[around(z_hi, step)], pair_recv.at[-step % RING])
+    got(amp_z.at[pl.ds(0, RING - 1)], pair_recv.at[0])
     put_rows(swap_order(take_rows(amp_z)), amp_cut_x)
     for step in far_first:
-        send_pair(1, amp_cut_x.at[around(x, step)], amp_x.at[x], 4 + step % RING, at_x(step))
+        send_pair(1, amp_cut_x.at[around(x, step)], amp_x.at[x], 4, at_x(step))
     amp_x[x] = amp_cut_x[x]
     join_from_partners([int_got[p] for p in range(GROUP)], turn.at[0], int_all.at[slot(1, oo)])
     spread_int(1)
@@ -243,20 +247,18 @@
     onward_int(0)
     relay_int(0, 0)
 
-    for step in near:
-        got(amp_x.at[around(x, step)], pair_recv.at[4 + -step % RING])
+    got(amp_x.at[pl.ds(0, RING - 1)], pair_recv.at[4])
     join_from_partners(take_rows(amp_x), turn.at[1], amp_all.at[slot(1, vv)])
     spread_amp(1)
     relay_int(0, 1)
     relay_int(0, -1)
-    relay_int(1, 0)
     onward_int(1, (1, -1))
-    relay_int(0, 2)
     onward_int(1, (2,))
+    corner_int()
     pass_direct()
     onward_amp(1)
     def finish(kind):
-        got(int_all.at[pl.ds(0, (8 if kind == 0 else 11) * CDS)], int_done.at[kind])
+        got(int_all.at[pl.ds(0, (9 if kind == 0 else 11) * CDS)], int_done.at[kind])
         got(amp_all.at[pl.ds(0, 8 * CDS)], amp_done.at[kind])
 
     finish(0)

time: 28.6 us -> 28.4 us (level)
  no operation moved by 1% of the time
where the time goes in v7:
time: 28.4 us; the launch traced here: 28.3 us
  Pallas kernels  28.3 us (100%)
    pallas_call x1, Pallas kernels, gathered(): pl.pallas_call(gather_kernel, out_shape=(whole, whole, square, square), i...  26.6 us
    pallas_call x1, Pallas kernels, ladder(): pl.pallas_call(ladder_kernel, out_shape=jax.ShapeDtypeStruct((WIDE, WIDE)...  1.69 us

profile of v7, /device:TPU:1, one launch (start us, length us, event | category | flops | bytes accessed | tf_op | source)
XLA Modules:
  0.0 28.3 jit_solution(4770672009870007604)
XLA Ops:
  0.0 26.6 %gather_pairs.1 = (bf16[512,1024]{1,0:T(8,128)(2,1)S(1)}, bf16[512,1024]{1,0:T(8,128)(2,1)S(1)}, f32[1024,1024]{1,0:T(8,128)S(1)}, f32[1024,1024]{1,0:T(8,128)S(1)}) custom-call(bf16[16,1024]{1,0:T(8,128)(2,1)} %bitcast.3, bf16[16,1024]{1,0:T(8,128)(2,1)} %amp_in.1, f32[1,128]{1,0:T(1,128)} %bitcast.4, f32[1,128]{1,0:T(1,128)} %bitcast.5), custom_call_target="tpu_custom_call" | custom-call | tf_op jit(solution)/shard_map/gather_pairs/pallas_call | solution.py:292
  26.6 1.7 %ladder_sum.1 = bf16[1024,1024]{1,0:T(8,128)(2,1)} custom-call(bf16[512,1024]{1,0:T(8,128)(2,1)S(1)} %get-tuple-element.9.int_ref, bf16[512,1024]{1,0:T(8,128)(2,1)S(1)} %get-tuple-element.10.amp_ref, f32[1024,1024]{1,0:T(8,128)S(1)} %get-tuple-element.11.inverse, f32[1024,1024]{1,0:T(8,128)S(1)} %get-tuple-element.12.partial), custom_call_target="tpu_custom_call" | custom-call | tf_op jit(solution)/shard_map/ladder_sum/pallas_call | solution.py:327
